TPU v7x, 256 devices: a whole 4x4x8 slice. The times are simulated.
256 devices in a mesh: gx: 8 (over x, core), gy: 32 (over y, z).
Axes of the slice: x: 4, y: 4, z: 8, core: 2. Of those that a mesh axis runs over, the one named last changes fastest.
Arguments:
- leaf_multipoles: bfloat16 [32, 128, 16, 128], P('gx', 'gy'), may hold values from -6 to 6
- top_local: float32 [2, 8, 1, 128], replicated, may hold values from -6 to 6
- upward_ops: bfloat16 [1024, 128], replicated, may hold values from -0.1875 to 0.1875
- downward_ops: bfloat16 [128, 1024], replicated, may hold values from -0.5 to 0.5
- translate_ops: bfloat16 [316, 128, 128], replicated, may hold values from -0.0390625 to 0.0390625
- interaction_leaf: int32 [316, 32, 128, 16], P(None, 'gx', 'gy'), may hold values from 0 to 1, as said below
- interaction_one: int32 [316, 16, 64, 8], P(None, 'gx', 'gy'), may hold values from 0 to 1, as said below
- interaction_two: int32 [316, 8, 32, 4], P(None, 'gx', 'gy'), may hold values from 0 to 1, as said below
- interaction_three: int32 [316, 4, 16, 2], replicated, may hold values from 0 to 1, as said below
Outputs:
- leaf_local: float32 [32, 128, 16, 128], P('gx', 'gy')
- top_multipoles: bfloat16 [2, 8, 1, 128], replicated
Inputs may be any that keep to these rules, and one draw needn't show every extreme that they name: interaction_leaf[k, b] is 1 exactly when box b and the box at b + offset k are both occupied, lie in the grid, and the latter is a child of a neighbour of b's parent (or of that parent) without touching b; occupied boxes are drawn afresh. `interaction_one`: the same rule at level one, a box being occupied when one of its children is. `interaction_two`: the same rule at level two. `interaction_three`: the same rule at level three.
All inputs are finite; a program needn't handle non-finite values.
Results may differ from a plain program's by a relative error of at most 0.0075.
Values may be sent and summed in bfloat16 or wider, within the bound.
No kernel may reach another device: no remote copies, remote signals or barrier semaphores. Data moves between devices by JAX's collectives and lax.ppermute only.
A program may use at most 256 MiB of HBM per device.

v0:
```python
import functools

import jax
import jax.numpy as jnp
from jax import lax
from jax.experimental import pallas as pl
from jax.experimental.pallas import tpu as pltpu
from jax.sharding import PartitionSpec as P

F32 = jnp.float32
BF16 = jnp.bfloat16
COEF = 128
PAIR = 256
NOFF = 316
VM = pltpu.VMEM
ANY_SPEC = pl.BlockSpec(memory_space=pl.ANY)
VMEM_SPEC = pl.BlockSpec(memory_space=pltpu.VMEM)

PLANE_FIRST = (0, 49, 98, 138, 178, 218, 267)
PLANE_COUNT = (49, 49, 40, 40, 40, 49, 49)
THIN_FIRST = (0, 7, 14, 18, 22, 26, 33)


def dot(lhs, rhs):
    return jnp.dot(lhs, rhs, preferred_element_type=F32)


def prepare_kernel(
    leaf_ref, up_ref, list_leaf_ref, list_one_ref,
    leaf_out, leaf_mask_out, one_out, one_mask_out, even_out, odd_out, two_out,
    raw, masked, marks, one_raw, one_masked, one_marks, pairs, two_in,
):
    parity = lax.axis_index("gx") % 2
    for x in range(4):
        for y in range(4):
            rows = pl.ds((x * 4 + y) * 16, 16)
            flags = list_leaf_ref[x, y].astype(F32)
            mark = jnp.broadcast_to(jnp.max(flags, axis=1, keepdims=True), (16, COEF))
            value = leaf_ref[x, y].astype(F32)
            raw[rows, :] = value
            masked[rows, :] = value * mark
            marks[rows, :] = mark
    cols = []
    for p in range(2):
        for q in range(2):
            for r in range(2):
                parts = []
                for x in range(2):
                    for y in range(2):
                        first = ((2 * x + p) * 4 + 2 * y + q) * 16 + r
                        parts.append(raw[pl.ds(first, 8, stride=2), :])
                cols.append(jnp.concatenate(parts, axis=0).astype(BF16))
    level_one = dot(jnp.concatenate(cols, axis=1), up_ref[...]).astype(BF16).astype(F32)
    one_raw[...] = level_one
    for x in range(2):
        for y in range(2):
            rows = pl.ds((x * 2 + y) * 8, 8)
            flags = list_one_ref[x, y].astype(F32)
            mark = jnp.broadcast_to(jnp.max(flags, axis=1, keepdims=True), (8, COEF))
            one_masked[rows, :] = one_raw[rows, :] * mark
            one_marks[rows, :] = mark
    two_in[...] = jnp.zeros_like(two_in)
    for p in range(2):
        for q in range(2):
            for r in range(2):
                first = (p * 2 + q) * 8 + r
                lane = (4 * p + 2 * q + r) * COEF
                two_in[0:4, lane:lane + COEF] = one_raw[pl.ds(first, 4, stride=2), :]
    level_two = dot(two_in[...].astype(BF16), up_ref[...])
    two_out[...] = level_two[0:4, :].astype(BF16)
    for x in range(4):
        for half in range(2):
            for r in range(2):
                lane = r * COEF
                parts = []
                part_marks = []
                for y in (2 * half, 2 * half + 1):
                    first = (x * 4 + y) * 16 + r
                    parts.append(masked[pl.ds(first, 8, stride=2), :])
                    part_marks.append(marks[pl.ds(first, 8, stride=2), :])
                rows = slice(half * 16, half * 16 + 16)
                leaf_out[x, rows, lane:lane + COEF] = jnp.concatenate(parts, axis=0).astype(BF16)
                leaf_mask_out[x, rows, lane:lane + COEF] = jnp.concatenate(part_marks, axis=0)
    for column in range(4):
        for r in range(2):
            lane = r * COEF
            rows = slice(column * 4, column * 4 + 4)
            pairs[rows, lane:lane + COEF] = one_masked[pl.ds(column * 8 + r, 4, stride=2), :]
            one_mask_out[rows, lane:lane + COEF] = one_marks[pl.ds(column * 8 + r, 4, stride=2), :]
    one_pairs = pairs[...].astype(BF16)
    one_out[...] = one_pairs
    for x in range(2):
        even_out[x * 32:x * 32 + 32, :] = leaf_out[2 * (1 - parity) + x]
        odd_out[x * 32:x * 32 + 32, :] = leaf_out[2 * parity + x]
    even_out[64:80, :] = one_pairs
    odd_out[64:80, :] = one_pairs


def prepare(leaf, upward_ops, list_leaf, list_one):
    return pl.pallas_call(
        prepare_kernel,
        out_shape=(
            jax.ShapeDtypeStruct((4, 32, PAIR), BF16),
            jax.ShapeDtypeStruct((4, 32, PAIR), F32),
            jax.ShapeDtypeStruct((16, PAIR), BF16),
            jax.ShapeDtypeStruct((16, PAIR), F32),
            jax.ShapeDtypeStruct((80, PAIR), BF16),
            jax.ShapeDtypeStruct((80, PAIR), BF16),
            jax.ShapeDtypeStruct((4, COEF), BF16),
        ),
        in_specs=[VMEM_SPEC] * 4,
        out_specs=[VMEM_SPEC] * 7,
        scratch_shapes=[
            VM((256, COEF), F32),
            VM((256, COEF), F32),
            VM((256, COEF), F32),
            VM((32, COEF), F32),
            VM((32, COEF), F32),
            VM((32, COEF), F32),
            VM((16, PAIR), F32),
            VM((8, 1024), F32),
        ],
        compiler_params=pltpu.CompilerParams(vmem_limit_bytes=16 * 2**20),
        name="prepare",
    )(leaf, upward_ops, list_leaf, list_one)


def forward_kernel(leaf_ref, one_ref, even_ref, odd_ref, even_out, odd_out):
    parity = lax.axis_index("gy") % 2
    for out, side in ((even_out, 1 - parity), (odd_out, parity)):
        rows = pl.ds(pl.multiple_of(side * 16, 16), 16)
        for x in range(4):
            out[x * 16:x * 16 + 16, :] = leaf_ref[x, rows, :]
        out[64:80, :] = one_ref[...]
        for place, got in enumerate((even_ref, odd_ref)):
            first = 80 + 48 * place
            for x in range(2):
                face = pl.ds(pl.multiple_of(x * 32 + side * 16, 16), 16)
                out[first + x * 16:first + x * 16 + 16, :] = got[face, :]
            out[first + 32:first + 48, :] = got[64:80, :]


def forward(leaf, one, even, odd):
    return pl.pallas_call(
        forward_kernel,
        out_shape=(jax.ShapeDtypeStruct((176, PAIR), BF16),) * 2,
        in_specs=[VMEM_SPEC] * 4,
        out_specs=[VMEM_SPEC] * 2,
        compiler_params=pltpu.CompilerParams(vmem_limit_bytes=4 * 2**20),
        name="forward",
    )(leaf, one, even, odd)


def lane_of(plane, b, c):
    if plane in (2, 3, 4) and -1 <= b <= 1:
        return PLANE_FIRST[plane] + THIN_FIRST[b + 3] + {-3: 0, -2: 1, -1: 2, 2: 2, 3: 3}[c]
    first = THIN_FIRST[b + 3] if plane in (2, 3, 4) else 7 * (b + 3)
    return PLANE_FIRST[plane] + first + c + 3


def window_of(window, one_window, leaf_ref, one_ref, evenx_ref, oddx_ref, eveny_ref, oddy_ref):
    parity_x = lax.axis_index("gx") % 2
    parity_y = lax.axis_index("gy") % 2
    even_x, odd_x = 6 * (1 - parity_x), 6 * parity_x
    even_y, odd_y = 6 * (1 - parity_y), 6 * parity_y
    one_even_x, one_odd_x = 1 + 4 * (1 - parity_x), 1 + 4 * parity_x
    one_even_y, one_odd_y = 1 + 4 * (1 - parity_y), 1 + 4 * parity_y

    def put(x, y, block):
        block = block.astype(F32)
        window[x, y, 8:16, :] = block[0:8]
        window[x, y + 1, 8:16, :] = block[8:16]

    def put_one(x, y, block):
        block = block.astype(F32)
        for i in range(2):
            for j in range(2):
                first = (2 * i + j) * 4
                one_window[x + i, y + j, 8:12, :] = block[first:first + 4]

    for x in range(4):
        put(2 + x, 2, leaf_ref[x, 0:16, :])
        put(2 + x, 4, leaf_ref[x, 16:32, :])
    put_one(3, 3, one_ref[...])
    for got, place, one_place in ((evenx_ref, even_x, one_even_x), (oddx_ref, odd_x, one_odd_x)):
        for x in range(2):
            put(place + x, 2, got[x * 32:x * 32 + 16, :])
            put(place + x, 4, got[x * 32 + 16:x * 32 + 32, :])
        put_one(one_place, 3, got[64:80, :])
    for got, y, one_y in ((eveny_ref, even_y, one_even_y), (oddy_ref, odd_y, one_odd_y)):
        for x in range(4):
            put(2 + x, y, got[x * 16:x * 16 + 16, :])
        put_one(3, one_y, got[64:80, :])
        for first, place, one_place in ((80, even_x, one_even_x), (128, odd_x, one_odd_x)):
            for x in range(2):
                put(place + x, y, got[first + x * 16:first + x * 16 + 16, :])
            put_one(one_place, one_y, got[first + 32:first + 48, :])


def translate_kernel(
    leaf_ref, leaf_mask_ref, one_ref, one_mask_ref, evenx_ref, oddx_ref, eveny_ref, oddy_ref,
    two_ref, up_ref, down_ref, top_ref, list_two_ref, list_three_ref, ops_hbm,
    out_ref, top_out,
    ops, window, one_window, chunks, one_chunks, high_chunks, two_rows, three_rows, acc,
    flags, one_local, sems,
):
    gx = lax.axis_index("gx")
    gy = lax.axis_index("gy")
    copies = []
    for plane in range(7):
        span = pl.ds(PLANE_FIRST[plane], PLANE_COUNT[plane])
        copies.append(pltpu.make_async_copy(ops_hbm.at[span], ops.at[span], sems.at[plane]))
        copies[-1].start()

    window[:, :, 0:8, :] = jnp.zeros((8, 8, 8, PAIR), F32)
    window[:, :, 16:24, :] = jnp.zeros((8, 8, 8, PAIR), F32)
    one_window[...] = jnp.zeros_like(one_window)
    window_of(window, one_window, leaf_ref, one_ref, evenx_ref, oddx_ref, eveny_ref, oddy_ref)
    chunks[...] = jnp.zeros_like(chunks)

    def fill(x, carry):
        for q in range(2):
            for d in range(3):
                for shift in range(3):
                    rows = pl.ds(7 + shift, 8)
                    both = [window[x, 2 * (y + d) + q, rows, :] for y in range(2)]
                    chunks[x, 3 * q + d, shift] = jnp.concatenate(both, axis=0).astype(BF16)
        return carry

    lax.fori_loop(0, 8, fill, 0)

    two_rows[...] = two_ref[...].astype(F32)
    cols = []
    for p in range(2):
        for q in range(2):
            for r in range(2):
                parts = []
                for x in range(4):
                    for z in range(2):
                        first = (2 * x + p) * 128 + q * 4 + 2 * z + r
                        parts.append(two_rows[pl.ds(first, 16, stride=8), :])
                cols.append(jnp.concatenate(parts, axis=0).astype(BF16))
    level_three = dot(jnp.concatenate(cols, axis=1), up_ref[...])
    three_rows[...] = level_three.astype(BF16).astype(F32)
    cols = []
    for p in range(2):
        for q in range(2):
            for r in range(2):
                parts = []
                for x in range(2):
                    first = ((2 * x + p) * 2 + r) * 16 + q
                    parts.append(three_rows[pl.ds(first, 8, stride=2), :])
                cols.append(jnp.concatenate(parts, axis=0).astype(BF16))
    top_out[...] = dot(jnp.concatenate(cols, axis=1), up_ref[...]).astype(BF16)

    three_x, three_y = gx // 2, gy // 2
    flags[...] = jnp.zeros_like(flags)
    flags[0:4, :] = list_two_ref[...].astype(F32)
    flags[4:6, :] = list_three_ref[three_x, three_y].astype(F32)
    row = lax.broadcasted_iota(jnp.int32, (8, NOFF), 0)
    held = flags[...]
    moved = jnp.concatenate([jnp.zeros((8, 1), F32), held[:, :NOFF - 1]], axis=1)
    marked = jnp.where(row % 2 == 0, held, moved)
    row = lax.broadcasted_iota(jnp.int32, (8, COEF), 0)
    for plane in range(7):
        two_x = jnp.clip(gx + plane - 3, 0, 7)
        far_x = jnp.clip(three_x + plane - 3, 0, 3)
        for b in range(-3, 4):
            two_first = (two_x * 32 + jnp.clip(gy + b, 0, 31)) * 4
            far_first = far_x * 32 + jnp.clip(three_y + b, 0, 15)
            thin = plane in (2, 3, 4) and -1 <= b <= 1
            for r in range(2):
                low = two_rows[pl.ds(two_first + r, 1), :]
                high = two_rows[pl.ds(two_first + 2 + r, 1), :]
                far = three_rows[pl.ds(far_first + 16 * r, 1), :]
                low, high, far = (jnp.broadcast_to(v, (8, COEF)) for v in (low, high, far))
                near = jnp.where(row < 2, low, jnp.where(row < 4, high, far))
                for shift in range(3):
                    if thin and shift == 1:
                        continue
                    lane = lane_of(plane, b, 2 * (shift - 1) + r)
                    mark = jnp.broadcast_to(marked[:, lane:lane + 1], (8, COEF))
                    if shift == 0:
                        value = low
                    elif shift == 2:
                        value = high
                    else:
                        value = near
                    value = jnp.concatenate([value * mark, jnp.zeros((8, COEF), F32)], axis=0)
                    high_chunks[plane * 7 + b + 3, shift, :, r * COEF:r * COEF + COEF] = (
                        value.astype(BF16)
                    )

    acc[...] = jnp.zeros_like(acc)
    zero = jnp.zeros((COEF, COEF), BF16)

    def plane_step(plane, first, thin_plane):
        a = plane - 3
        places = []
        for px in range(2):
            good = (a >= -2) if px == 0 else (a <= 2)
            for x in range(2):
                places.append(jnp.where(good, 2 * x + px + a + 2, 8))
        for b in range(-3, 4):
            for shift in range(3):
                for px in range(2):
                    for py in range(2):
                        rows = slice((2 * px + py) * 4, (2 * px + py) * 4 + 4)
                        one_chunks[b + 3, shift, rows, :] = one_window[
                            px + a + 3, py + b + 3, 7 + shift:11 + shift, :
                        ]
        total = None
        for b in range(-3, 4):
            thin = thin_plane and -1 <= b <= 1
            start = first + (THIN_FIRST[b + 3] if thin_plane else 7 * (b + 3))
            shifts = (0, 2) if thin else (0, 1, 2)
            left = []
            right = []
            for shift in shifts:
                blocks = []
                for px in range(2):
                    for py in range(2):
                        y = py + b
                        good = (b >= -2) if py == 0 else (b <= 2)
                        q, d = y % 2, y // 2 + 1
                        for x in range(2):
                            if good:
                                blocks.append(chunks[places[2 * px + x], 3 * q + d, shift])
                            else:
                                blocks.append(jnp.zeros((16, PAIR), BF16))
                blocks.append(one_chunks[b + 3, shift].astype(BF16))
                blocks.append(high_chunks[plane * 7 + b + 3, shift])
                left.append(jnp.concatenate(blocks, axis=0))
                if thin:
                    if shift == 0:
                        same, prev, after = ops[start + 1], ops[start], zero
                    else:
                        same, prev, after = ops[start + 2], zero, ops[start + 3]
                else:
                    c = 2 * (shift - 1) + 3
                    same, prev, after = ops[start + c], ops[start + c - 1], ops[start + c + 1]
                right.append(jnp.concatenate([same, prev], axis=1))
                right.append(jnp.concatenate([after, same], axis=1))
            product = dot(jnp.concatenate(left, axis=1), jnp.concatenate(right, axis=0))
            total = product if total is None else total + product
        acc[...] = acc[...] + total

    def wide_step(i, carry):
        plane = jnp.where(i < 2, i, i + 3)
        first = jnp.where(i < 2, 49 * i, 49 * i + 120)
        span = pl.ds(first, 49)
        pltpu.make_async_copy(ops_hbm.at[span], ops.at[span], sems.at[plane]).wait()
        plane_step(plane, first, False)
        return carry

    def thin_step(i, carry):
        first = 98 + 40 * i
        span = pl.ds(first, 40)
        pltpu.make_async_copy(ops_hbm.at[span], ops.at[span], sems.at[i + 2]).wait()
        plane_step(i + 2, first, True)
        return carry

    lax.fori_loop(0, 3, thin_step, 0)
    lax.fori_loop(0, 4, wide_step, 0)

    high = acc[144:152, :]
    top_x, top_y = three_x // 2, three_y // 2
    column = pl.multiple_of((three_x % 2 * 4 + three_y % 2 * 2) * COEF, PAIR)
    top_row = jnp.broadcast_to(top_ref[top_x, top_y], (8, COEF)).astype(BF16)
    three = dot(top_row, down_ref[:, pl.ds(column, PAIR)])
    row = lax.broadcasted_iota(jnp.int32, (8, COEF), 0)
    three_low = three[0:1, 0:COEF] + high[4:5, 0:COEF] * 0.125
    three_high = three[0:1, COEF:PAIR] + high[5:6, COEF:PAIR] * 0.125
    local_three = jnp.where(
        row == 0, jnp.broadcast_to(three_low, (8, COEF)), jnp.broadcast_to(three_high, (8, COEF))
    )
    column = pl.multiple_of((gx % 2 * 4 + gy % 2 * 2) * COEF, PAIR)
    two = dot(local_three.astype(BF16), down_ref[:, pl.ds(column, PAIR)])
    local_two = None
    for z in range(4):
        lanes = slice((z % 2) * COEF, (z % 2) * COEF + COEF)
        value = two[z // 2:z // 2 + 1, lanes] + high[z:z + 1, lanes] * 0.25
        value = jnp.broadcast_to(value, (8, COEF))
        local_two = value if local_two is None else jnp.where(row >= z, value, local_two)
    one = dot(local_two.astype(BF16), down_ref[...])
    for column in range(4):
        rows = slice(column * 4, column * 4 + 4)
        for r in range(2):
            lanes = slice(r * COEF, r * COEF + COEF)
            wide = slice((2 * column + r) * COEF, (2 * column + r) * COEF + COEF)
            far = acc[128 + column * 4:132 + column * 4, lanes] * one_mask_ref[rows, lanes]
            one_local[pl.ds(column * 8 + r, 4, stride=2), :] = one[0:4, wide] + far * 0.5
    leaf = dot(one_local[...].astype(BF16), down_ref[...])
    for px in range(2):
        for py in range(2):
            for x in range(2):
                for y in range(2):
                    part = 8 * (2 * x + y)
                    held = ((2 * px + py) * 2 + x) * 16 + 8 * y
                    box_x, box_y = 2 * x + px, 2 * y + py
                    for r in range(2):
                        lanes = slice(r * COEF, r * COEF + COEF)
                        wide = slice((4 * px + 2 * py + r) * COEF, (4 * px + 2 * py + r + 1) * COEF)
                        mark = leaf_mask_ref[box_x, box_y * 8:box_y * 8 + 8, lanes]
                        out_ref[box_x, box_y, pl.ds(r, 8, stride=2), :] = (
                            leaf[part:part + 8, wide] + acc[held:held + 8, lanes] * mark
                        )


def translate(*operands):
    return pl.pallas_call(
        translate_kernel,
        out_shape=(
            jax.ShapeDtypeStruct((4, 4, 16, COEF), F32),
            jax.ShapeDtypeStruct((16, COEF), BF16),
        ),
        in_specs=[VMEM_SPEC] * 14 + [ANY_SPEC],
        out_specs=[VMEM_SPEC] * 2,
        scratch_shapes=[
            VM((NOFF, COEF, COEF), BF16),
            VM((8, 8, 24, PAIR), F32),
            VM((8, 8, 16, PAIR), F32),
            VM((9, 6, 3, 16, PAIR), BF16),
            VM((7, 3, 16, PAIR), F32),
            VM((49, 3, 16, PAIR), BF16),
            VM((1024, COEF), F32),
            VM((128, COEF), F32),
            VM((160, PAIR), F32),
            VM((8, NOFF), F32),
            VM((32, COEF), F32),
            pltpu.SemaphoreType.DMA((7,)),
        ],
        compiler_params=pltpu.CompilerParams(vmem_limit_bytes=40 * 2**20),
        name="translate",
    )(*operands)


def swaps(count):
    even = [(i, i ^ 1) for i in range(count)]
    odd = [(i, ((i + 1) ^ 1) - 1) for i in range(1, count - 1)]
    return even, odd


def local(
    leaf_multipoles, top_local, upward_ops, downward_ops, translate_ops,
    interaction_leaf, interaction_one, interaction_two, interaction_three,
):
    count_x, count_y = lax.axis_size("gx"), lax.axis_size("gy")
    last = (1, 2, 3, 0)
    leaf, leaf_mask, one, one_mask, to_even, to_odd, two = prepare(
        leaf_multipoles, upward_ops, interaction_leaf.transpose(last), interaction_one.transpose(last)
    )
    even, odd = swaps(count_x)
    even_x = lax.ppermute(to_even, "gx", even)
    odd_x = lax.ppermute(to_odd, "gx", odd)
    to_even, to_odd = forward(leaf, one, even_x, odd_x)
    even, odd = swaps(count_y)
    even_y = lax.ppermute(to_even, "gy", even)
    odd_y = lax.ppermute(to_odd, "gy", odd)
    copies = jnp.broadcast_to(two[None], (count_x * count_y, 4, COEF))
    all_two = lax.all_to_all(copies, ("gx", "gy"), 0, 0, tiled=True).reshape(-1, COEF)
    leaf_local, top = translate(
        leaf, leaf_mask, one, one_mask, even_x, odd_x, even_y, odd_y,
        all_two, upward_ops, downward_ops, top_local,
        interaction_two.transpose(last).reshape(4, NOFF), interaction_three.transpose(last),
        translate_ops,
    )
    return leaf_local, top.reshape(2, 8, 1, COEF)


def solution(mesh):
    return jax.shard_map(
        local,
        mesh=mesh,
        in_specs=(
            P("gx", "gy", None, None),
            P(),
            P(),
            P(),
            P(),
            P(None, "gx", "gy", None),
            P(None, "gx", "gy", None),
            P(None, "gx", "gy", None),
            P(),
        ),
        out_specs=(P("gx", "gy", None, None), P()),
        check_vma=False,
    )
```

profile of v0, /device:TPU:1, one launch (start us, length us, event | category | flops | bytes accessed | tf_op | source)
XLA Modules:
  0.0 52.4 jit_solution(6077489642718665447)
XLA Ops:
  0.6 0.0 copy-start.1
  0.6 0.9 %copy-done.1 = bf16[1024,128]{1,0:T(8,128)(2,1)S(1)} copy-done((bf16[1024,128]{1,0:T(8,128)(2,1)S(1)}, bf16[1024,128]{1,0:T(8,128)(2,1)}, u32[]{:S(2)}) %copy-start.1) | copy-done | bytes 262168
  1.6 1.0 %copy-done.3 = s32[316,4,4,16]{0,3,2,1:T(8,128)S(1)} copy-done((s32[316,4,4,16]{0,3,2,1:T(8,128)S(1)}, s32[316,4,4,16]{0,3,2,1:T(8,128)}, u32[]{:S(2)}) %copy-start.3) | copy-done | bytes 323608
  2.6 0.8 %copy-done.6 = bf16[4,4,16,128]{3,2,1,0:T(8,128)(2,1)S(1)} copy-done((bf16[4,4,16,128]{3,2,1,0:T(8,128)(2,1)S(1)}, bf16[4,4,16,128]{3,2,1,0:T(8,128)(2,1)}, u32[]{:S(2)}) %copy-start.6) | copy-done | bytes 65560
  3.4 0.8 %copy-done.7 = s32[316,2,2,8]{0,3,2,1:T(8,128)S(1)} copy-done((s32[316,2,2,8]{0,3,2,1:T(8,128)S(1)}, s32[316,2,2,8]{0,3,2,1:T(8,128)}, u32[]{:S(2)}) %copy-start.7) | copy-done | bytes 40472
  4.2 0.3 prepare.1
  4.6 0.8 %broadcast_in_dim.2 = bf16[256,4,128]{2,1,0:T(4,128)(2,1)} broadcast(bf16[4,128]{1,0:T(4,128)(2,1)S(1)} %get-tuple-element.21), dimensions={1,2} | broadcast | bytes 263168 | tf_op jit(solution)/shard_map/broadcast_in_dim | solution.py:460
  5.3 15.7 %all-to-all-start = ((bf16[256,4,128]{2,1,0:T(4,128)(2,1)}), bf16[256,4,128]{2,1,0:T(4,128)(2,1)S(1)}, u32[]{:S(2)}, u32[]{:S(2)}) async-start(bf16[256,4,128]{2,1,0:T(4,128)(2,1)} %broadcast_in_dim.2), calls=%async_computation | async-start | bytes 524288 | tf_op jit(solution)/shard_map/all_to_all | solution.py:461
  21.0 2.2 %collective-permute-start = (bf16[80,256]{1,0:T(8,128)(2,1)S(1)}, bf16[80,256]{1,0:T(8,128)(2,1)S(1)}, u32[]{:S(2)}, u32[]{:S(2)}) collective-permute-start(bf16[80,256]{1,0:T(8,128)(2,1)S(1)} %get-tuple-element.17), channel_id=1, source_target_pairs={{0,32},{32,0},{64,96},{96,64},{128,160},{160,128},{192,224},{224,1... | collective-permute-start | bytes 122888 | tf_op jit(solution)/shard_map/ppermute | solution.py:454
  23.2 1.9 %collective-permute-start.1 = (bf16[80,256]{1,0:T(8,128)(2,1)S(1)}, bf16[80,256]{1,0:T(8,128)(2,1)S(1)}, u32[]{:S(2)}, u32[]{:S(2)}) collective-permute-start(bf16[80,256]{1,0:T(8,128)(2,1)S(1)} %get-tuple-element.18), channel_id=1, source_target_pairs={{32,64},{64,32},{96,128},{128,96},{160,192},{192,160},{33,65},{65,... | collective-permute-start | bytes 122888 | tf_op jit(solution)/shard_map/ppermute | solution.py:455
  25.2 0.0 collective-permute-done.even_ref.evenx_ref
  25.2 3.9 %collective-permute-done.1.odd_ref.oddx_ref = bf16[80,256]{1,0:T(8,128)(2,1)S(1)} collective-permute-done((bf16[80,256]{1,0:T(8,128)(2,1)S(1)}, bf16[80,256]{1,0:T(8,128)(2,1)S(1)}, u32[]{:S(2)}, u32[]{:S(2)}) %collective-permute-start.1) | collective-permute-done | bytes 40992 | tf_op jit(solution)/shard_map/ppermute | solution.py:455
  29.1 0.1 collective-permute-start.2
  29.2 0.7 %collective-permute-start.3 = (bf16[176,256]{1,0:T(8,128)(2,1)S(1)}, bf16[176,256]{1,0:T(8,128)(2,1)S(1)}, u32[]{:S(2)}, u32[]{:S(2)}) collective-permute-start(bf16[176,256]{1,0:T(8,128)(2,1)S(1)} %get-tuple-element.20), channel_id=1, source_target_pairs={{1,2},{2,1},{3,4},{4,3},{5,6},{6,5},{7,8},{8,7},{9,10},{10,9},{11,... | collective-permute-start | bytes 270344 | tf_op jit(solution)/shard_map/ppermute | solution.py:459
  29.8 3.0 %collective-permute-done.2.eveny_ref = bf16[176,256]{1,0:T(8,128)(2,1)S(1)} collective-permute-done((bf16[176,256]{1,0:T(8,128)(2,1)S(1)}, bf16[176,256]{1,0:T(8,128)(2,1)S(1)}, u32[]{:S(2)}, u32[]{:S(2)}) %collective-permute-start.2) | collective-permute-done | bytes 90144 | tf_op jit(solution)/shard_map/ppermute | solution.py:458
  32.8 0.0 collective-permute-done.3.oddy_ref
  32.8 4.0 %all-to-all-done = bf16[256,4,128]{2,1,0:T(4,128)(2,1)S(1)} async-done(((bf16[256,4,128]{2,1,0:T(4,128)(2,1)}), bf16[256,4,128]{2,1,0:T(4,128)(2,1)S(1)}, u32[]{:S(2)}, u32[]{:S(2)}) %all-to-all-start) | async-done | bytes 262176 | tf_op jit(solution)/shard_map/all_to_all | solution.py:461
  36.8 3.9 %copy-done = bf16[316,128,128]{2,1,0:T(8,128)(2,1)S(1)} copy-done((bf16[316,128,128]{2,1,0:T(8,128)(2,1)S(1)}, bf16[316,128,128]{2,1,0:T(8,128)(2,1)}, u32[]{:S(2)}) %copy-start) | copy-done | bytes 10354712
  40.7 0.9 %copy-done.2 = bf16[1024,128]{1,0:T(8,128)(2,1)S(1)} copy-done((bf16[1024,128]{1,0:T(8,128)(2,1)S(1)}, bf16[1024,128]{1,0:T(8,128)(2,1)}, u32[]{:S(2)}) %copy-start.2) | copy-done | bytes 262168
  41.7 0.9 %copy-done.4 = bf16[128,1024]{1,0:T(8,128)(2,1)S(1)} copy-done((bf16[128,1024]{1,0:T(8,128)(2,1)S(1)}, bf16[128,1024]{1,0:T(8,128)(2,1)}, u32[]{:S(2)}) %copy-start.4) | copy-done | bytes 262168
  42.6 0.9 %copy-done.5 = s32[316,4,16,2]{0,3,2,1:T(2,128)S(1)} copy-done((s32[316,4,16,2]{0,3,2,1:T(2,128)S(1)}, s32[316,4,16,2]{0,3,2,1:T(2,128)}, u32[]{:S(2)}) %copy-start.5) | copy-done | bytes 161816
  43.6 0.7 %copy-done.8 = f32[2,8,1,128]{3,2,1,0:T(1,128)S(1)} copy-done((f32[2,8,1,128]{3,2,1,0:T(1,128)S(1)}, f32[2,8,1,128]{3,2,1,0:T(1,128)}, u32[]{:S(2)}) %copy-start.8) | copy-done | bytes 8216
  44.3 0.7 %copy-done.9 = s32[316,1,1,4]{0,3,2,1:T(4,128)S(1)} copy-done((s32[316,1,1,4]{0,3,2,1:T(4,128)S(1)}, s32[316,1,1,4]{0,3,2,1:T(4,128)}, u32[]{:S(2)}) %copy-start.9) | copy-done | bytes 5080
  45.0 7.5 %translate.1 = (f32[4,4,16,128]{3,2,1,0:T(8,128)}, bf16[16,128]{1,0:T(8,128)(2,1)}) custom-call(bf16[4,32,256]{2,1,0:T(8,128)(2,1)S(1)} %get-tuple-element.13.leaf_ref, f32[4,32,256]{2,1,0:T(8,128)S(1)} %get-tuple-element.14.leaf_mask_ref, bf16[16,256]{1,0:T(8,128)(2,1)S(1)} %get-tuple-element.15.one_ref, f32[16,256]{1,0:T(8,128)S(1)} %get-tuple-element.16.one_mask_ref, ...), custom_call_target="tpu_custom_call" | custom-call | tf_op jit(solution)/shard_map/translate/pallas_call | solution.py:411
  (10 shorter events, 0.0 us)
Async XLA Ops:
  0.6 1.0 %copy-start.1 = (bf16[1024,128]{1,0:T(8,128)(2,1)S(1)}, bf16[1024,128]{1,0:T(8,128)(2,1)}, u32[]{:S(2)}) copy-start(bf16[1024,128]{1,0:T(8,128)(2,1)} %up_ref.3) | copy-start | bytes 786436
  1.6 1.0 %copy-start.3 = (s32[316,4,4,16]{0,3,2,1:T(8,128)S(1)}, s32[316,4,4,16]{0,3,2,1:T(8,128)}, u32[]{:S(2)}) copy-start(s32[316,4,4,16]{0,3,2,1:T(8,128)} %param.14) | copy-start | bytes 970756
  2.6 0.8 %copy-start.6 = (bf16[4,4,16,128]{3,2,1,0:T(8,128)(2,1)S(1)}, bf16[4,4,16,128]{3,2,1,0:T(8,128)(2,1)}, u32[]{:S(2)}) copy-start(bf16[4,4,16,128]{3,2,1,0:T(8,128)(2,1)} %leaf_ref.1) | copy-start | bytes 196612
  3.4 0.8 %copy-start.7 = (s32[316,2,2,8]{0,3,2,1:T(8,128)S(1)}, s32[316,2,2,8]{0,3,2,1:T(8,128)}, u32[]{:S(2)}) copy-start(s32[316,2,2,8]{0,3,2,1:T(8,128)} %param.15) | copy-start | bytes 121348
  5.3 31.5 %all-to-all-start = ((bf16[256,4,128]{2,1,0:T(4,128)(2,1)}), bf16[256,4,128]{2,1,0:T(4,128)(2,1)S(1)}, u32[]{:S(2)}, u32[]{:S(2)}) async-start(bf16[256,4,128]{2,1,0:T(4,128)(2,1)} %broadcast_in_dim.2), calls=%async_computation | async-start | bytes 524288 | tf_op jit(solution)/shard_map/all_to_all | solution.py:461
  21.0 4.2 %collective-permute-start = (bf16[80,256]{1,0:T(8,128)(2,1)S(1)}, bf16[80,256]{1,0:T(8,128)(2,1)S(1)}, u32[]{:S(2)}, u32[]{:S(2)}) collective-permute-start(bf16[80,256]{1,0:T(8,128)(2,1)S(1)} %get-tuple-element.17), channel_id=1, source_target_pairs={{0,32},{32,0},{64,96},{96,64},{128,160},{160,128},{192,224},{224,1... | collective-permute-start | bytes 122888 | tf_op jit(solution)/shard_map/ppermute | solution.py:454
  23.2 5.8 %collective-permute-start.1 = (bf16[80,256]{1,0:T(8,128)(2,1)S(1)}, bf16[80,256]{1,0:T(8,128)(2,1)S(1)}, u32[]{:S(2)}, u32[]{:S(2)}) collective-permute-start(bf16[80,256]{1,0:T(8,128)(2,1)S(1)} %get-tuple-element.18), channel_id=1, source_target_pairs={{32,64},{64,32},{96,128},{128,96},{160,192},{192,160},{33,65},{65,... | collective-permute-start | bytes 122888 | tf_op jit(solution)/shard_map/ppermute | solution.py:455
  29.1 3.8 %collective-permute-start.2 = (bf16[176,256]{1,0:T(8,128)(2,1)S(1)}, bf16[176,256]{1,0:T(8,128)(2,1)S(1)}, u32[]{:S(2)}, u32[]{:S(2)}) collective-permute-start(bf16[176,256]{1,0:T(8,128)(2,1)S(1)} %get-tuple-element.19), channel_id=1, source_target_pairs={{0,1},{1,0},{2,3},{3,2},{4,5},{5,4},{6,7},{7,6},{8,9},{9,8},{10,11... | collective-permute-start | bytes 270344 | tf_op jit(solution)/shard_map/ppermute | solution.py:458
  29.2 3.7 %collective-permute-start.3 = (bf16[176,256]{1,0:T(8,128)(2,1)S(1)}, bf16[176,256]{1,0:T(8,128)(2,1)S(1)}, u32[]{:S(2)}, u32[]{:S(2)}) collective-permute-start(bf16[176,256]{1,0:T(8,128)(2,1)S(1)} %get-tuple-element.20), channel_id=1, source_target_pairs={{1,2},{2,1},{3,4},{4,3},{5,6},{6,5},{7,8},{8,7},{9,10},{10,9},{11,... | collective-permute-start | bytes 270344 | tf_op jit(solution)/shard_map/ppermute | solution.py:459
  36.8 3.9 %copy-start = (bf16[316,128,128]{2,1,0:T(8,128)(2,1)S(1)}, bf16[316,128,128]{2,1,0:T(8,128)(2,1)}, u32[]{:S(2)}) copy-start(bf16[316,128,128]{2,1,0:T(8,128)(2,1)} %ops_hbm.1) | copy-start | bytes 31064068
  40.7 0.9 %copy-start.2 = (bf16[1024,128]{1,0:T(8,128)(2,1)S(1)}, bf16[1024,128]{1,0:T(8,128)(2,1)}, u32[]{:S(2)}) copy-start(bf16[1024,128]{1,0:T(8,128)(2,1)} %up_ref.3) | copy-start | bytes 786436
  41.7 0.9 %copy-start.4 = (bf16[128,1024]{1,0:T(8,128)(2,1)S(1)}, bf16[128,1024]{1,0:T(8,128)(2,1)}, u32[]{:S(2)}) copy-start(bf16[128,1024]{1,0:T(8,128)(2,1)} %down_ref.1) | copy-start | bytes 786436
  42.6 0.9 %copy-start.5 = (s32[316,4,16,2]{0,3,2,1:T(2,128)S(1)}, s32[316,4,16,2]{0,3,2,1:T(2,128)}, u32[]{:S(2)}) copy-start(s32[316,4,16,2]{0,3,2,1:T(2,128)} %param.17) | copy-start | bytes 485380
  43.6 0.7 %copy-start.8 = (f32[2,8,1,128]{3,2,1,0:T(1,128)S(1)}, f32[2,8,1,128]{3,2,1,0:T(1,128)}, u32[]{:S(2)}) copy-start(f32[2,8,1,128]{3,2,1,0:T(1,128)} %top_ref.1) | copy-start | bytes 24580
  44.3 0.7 %copy-start.9 = (s32[316,1,1,4]{0,3,2,1:T(4,128)S(1)}, s32[316,1,1,4]{0,3,2,1:T(4,128)}, u32[]{:S(2)}) copy-start(s32[316,1,1,4]{0,3,2,1:T(4,128)} %param.16) | copy-start | bytes 15172
where the time goes:
time: 53 us; the launch traced here: 52.4 us
  starting transfers between devices  20.6 us (39%)
  local copies, waits for them, and re-layouts  12.5 us (24%)
  waiting for transfers between devices  10.8 us (20%)
  Pallas kernels  7.82 us (15%)
  between operations  0.69 us (1%)
    all_to_all x1, starting transfers between devices, local(): lax.all_to_all(copies, ('gx', 'gy'), 0, 0, tiled=True).reshape(-1, COEF)  15.7 us
    unnamed x20, local copies, waits for them, and re-layouts  11.7 us
    pallas_call x1, Pallas kernels, translate(): pl.pallas_call(translate_kernel, out_shape=(jax.ShapeDtypeStruct((4, 4, 1...  7.48 us
    all_to_all x1, waiting for transfers between devices, local(): lax.all_to_all(copies, ('gx', 'gy'), 0, 0, tiled=True).reshape(-1, COEF)  3.96 us
    ppermute x1, waiting for transfers between devices, local(): odd_x = lax.ppermute(to_odd, 'gx', odd)  3.88 us
    ppermute x1, waiting for transfers between devices, local(): even_y = lax.ppermute(to_even, 'gy', even)  2.99 us
    ppermute x1, starting transfers between devices, local(): even_x = lax.ppermute(to_even, 'gx', even)  2.23 us
    ppermute x1, starting transfers between devices, local(): odd_x = lax.ppermute(to_odd, 'gx', odd)  1.91 us
  transfers between devices with their start and end apart: 5, of which 3 were waited for; matrix products, arithmetic and copies ran while one was open for 0% of the time, Pallas kernels for 0%

commit v1 on v0

v1 whole, which is shorter than its diff:
```python
import functools

import jax
import jax.numpy as jnp
from jax import lax
from jax.experimental import pallas as pl
from jax.experimental.pallas import tpu as pltpu
from jax.sharding import PartitionSpec as P

F32 = jnp.float32
BF16 = jnp.bfloat16
COEF = 128
PAIR = 256
NOFF = 316
VM = pltpu.VMEM
LIM1 = 60
LIM2 = 60
ANY_SPEC = pl.BlockSpec(memory_space=pl.ANY)
VMEM_SPEC = pl.BlockSpec(memory_space=pltpu.VMEM)

PLANE_FIRST = (0, 49, 98, 138, 178, 218, 267)
PLANE_COUNT = (49, 49, 40, 40, 40, 49, 49)
PLANE_ORDER = (2, 3, 4, 1, 5, 0, 6)
THIN_FIRST = (0, 7, 14, 18, 22, 26, 33)


def fetch(sources, targets, sems):
    copies = []
    for place, (source, target) in enumerate(zip(sources, targets)):
        copies.append(pltpu.make_async_copy(source, target, sems.at[place]))
        copies[-1].start()
    return copies


def dot(lhs, rhs):
    return jnp.dot(lhs, rhs, preferred_element_type=F32)


def prepare_kernel(
    leaf_hbm, up_hbm, list_leaf_hbm, list_one_hbm,
    own_out, even_out, odd_out, two_out,
    leaf_ref, up_ref, list_leaf_ref, list_one_ref,
    raw, masked, marks, one_raw, one_masked, one_marks, pairs, pair_marks, two_in, sems,
):
    copies = fetch(
        (leaf_hbm, list_leaf_hbm, up_hbm, list_one_hbm),
        (leaf_ref, list_leaf_ref, up_ref, list_one_ref),
        sems,
    )
    parity = lax.axis_index("gy") % 2
    copies[0].wait()
    copies[1].wait()
    for x in range(4):
        for y in range(4):
            rows = pl.ds((x * 4 + y) * 16, 16)
            flags = list_leaf_ref[x, y].astype(F32)
            mark = jnp.broadcast_to(jnp.max(flags, axis=1, keepdims=True), (16, COEF))
            value = leaf_ref[x, y].astype(F32)
            raw[rows, :] = value
            masked[rows, :] = value * mark
            marks[rows, :] = mark
    copies[2].wait()
    copies[3].wait()
    cols = []
    for p in range(2):
        for q in range(2):
            for r in range(2):
                parts = []
                for x in range(2):
                    for y in range(2):
                        first = ((2 * x + p) * 4 + 2 * y + q) * 16 + r
                        parts.append(raw[pl.ds(first, 8, stride=2), :])
                cols.append(jnp.concatenate(parts, axis=0).astype(BF16))
    level_one = dot(jnp.concatenate(cols, axis=1), up_ref[...]).astype(BF16).astype(F32)
    one_raw[...] = level_one
    for x in range(2):
        for y in range(2):
            rows = pl.ds((x * 2 + y) * 8, 8)
            flags = list_one_ref[x, y].astype(F32)
            mark = jnp.broadcast_to(jnp.max(flags, axis=1, keepdims=True), (8, COEF))
            one_masked[rows, :] = one_raw[rows, :] * mark
            one_marks[rows, :] = mark
    two_in[...] = jnp.zeros_like(two_in)
    for p in range(2):
        for q in range(2):
            for r in range(2):
                first = (p * 2 + q) * 8 + r
                lane = (4 * p + 2 * q + r) * COEF
                two_in[0:4, lane:lane + COEF] = one_raw[pl.ds(first, 4, stride=2), :]
    level_two = dot(two_in[...].astype(BF16), up_ref[...])
    two_out[...] = jnp.broadcast_to(level_two[0:4, :].astype(BF16)[None], two_out.shape)
    for x in range(4):
        for half in range(2):
            for r in range(2):
                lane = r * COEF
                parts = []
                part_marks = []
                for y in (2 * half, 2 * half + 1):
                    first = (x * 4 + y) * 16 + r
                    parts.append(masked[pl.ds(first, 8, stride=2), :])
                    part_marks.append(marks[pl.ds(first, 8, stride=2), :])
                first = x * 32 + half * 16
                rows = slice(first, first + 16)
                own_out[rows, lane:lane + COEF] = jnp.concatenate(parts, axis=0).astype(BF16)
                rows = slice(144 + first, 160 + first)
                own_out[rows, lane:lane + COEF] = jnp.concatenate(part_marks, axis=0).astype(BF16)
    for column in range(4):
        for r in range(2):
            lane = r * COEF
            rows = slice(column * 4, column * 4 + 4)
            pairs[rows, lane:lane + COEF] = one_masked[pl.ds(column * 8 + r, 4, stride=2), :]
            pair_marks[rows, lane:lane + COEF] = one_marks[pl.ds(column * 8 + r, 4, stride=2), :]
    one_pairs = pairs[...].astype(BF16)
    own_out[128:144, :] = one_pairs
    own_out[272:288, :] = pair_marks[...].astype(BF16)
    for out, side in ((even_out, 1 - parity), (odd_out, parity)):
        for x in range(4):
            rows = pl.ds(pl.multiple_of(x * 32 + side * 16, 16), 16)
            out[x * 16:x * 16 + 16, :] = own_out[rows, :]
    even_out[64:80, :] = one_pairs
    odd_out[64:80, :] = one_pairs


def prepare(receivers, leaf, upward_ops, list_leaf, list_one):
    return pl.pallas_call(
        prepare_kernel,
        out_shape=(
            jax.ShapeDtypeStruct((288, PAIR), BF16),
            jax.ShapeDtypeStruct((80, PAIR), BF16),
            jax.ShapeDtypeStruct((80, PAIR), BF16),
            jax.ShapeDtypeStruct((receivers, 4, COEF), BF16),
        ),
        in_specs=[ANY_SPEC] * 4,
        out_specs=[VMEM_SPEC] * 4,
        scratch_shapes=[
            VM((4, 4, 16, COEF), BF16),
            VM((1024, COEF), BF16),
            VM((4, 4, 16, NOFF), jnp.int32),
            VM((2, 2, 8, NOFF), jnp.int32),
            VM((256, COEF), F32),
            VM((256, COEF), F32),
            VM((256, COEF), F32),
            VM((32, COEF), F32),
            VM((32, COEF), F32),
            VM((32, COEF), F32),
            VM((16, PAIR), F32),
            VM((16, PAIR), F32),
            VM((8, 1024), F32),
            pltpu.SemaphoreType.DMA((4,)),
        ],
        compiler_params=pltpu.CompilerParams(vmem_limit_bytes=int(LIM1 * 2**20)),
        name="prepare",
    )(leaf, upward_ops, list_leaf, list_one)


def forward_kernel(own_ref, even_ref, odd_ref, even_out, odd_out):
    parity = lax.axis_index("gx") % 2
    for out, side in ((even_out, 1 - parity), (odd_out, parity)):
        out[0:64, :] = own_ref[pl.ds(pl.multiple_of(side * 64, 64), 64), :]
        out[64:80, :] = own_ref[128:144, :]
        for first, got in ((80, even_ref), (128, odd_ref)):
            out[first:first + 32, :] = got[pl.ds(pl.multiple_of(side * 32, 32), 32), :]
            out[first + 32:first + 48, :] = got[64:80, :]


def forward(own, even, odd):
    return pl.pallas_call(
        forward_kernel,
        out_shape=(jax.ShapeDtypeStruct((176, PAIR), BF16),) * 2,
        in_specs=[VMEM_SPEC] * 3,
        out_specs=[VMEM_SPEC] * 2,
        compiler_params=pltpu.CompilerParams(vmem_limit_bytes=4 * 2**20),
        cost_estimate=pl.CostEstimate(flops=2 * 10**11, bytes_accessed=10**9, transcendentals=0),
        name="forward",
    )(own, even, odd)


def lane_of(plane, b, c):
    if plane in (2, 3, 4) and -1 <= b <= 1:
        return PLANE_FIRST[plane] + THIN_FIRST[b + 3] + {-3: 0, -2: 1, -1: 2, 2: 2, 3: 3}[c]
    first = THIN_FIRST[b + 3] if plane in (2, 3, 4) else 7 * (b + 3)
    return PLANE_FIRST[plane] + first + c + 3


def window_of(window, one_window, own_ref, evenx_ref, oddx_ref, eveny_ref, oddy_ref):
    gx = lax.axis_index("gx")
    gy = lax.axis_index("gy")
    parity_x, parity_y = gx % 2, gy % 2
    even_x, odd_x = 6 * (1 - parity_x), 6 * parity_x
    even_y, odd_y = 6 * (1 - parity_y), 6 * parity_y
    one_even_x, one_odd_x = 1 + 4 * (1 - parity_x), 1 + 4 * parity_x
    one_even_y, one_odd_y = 1 + 4 * (1 - parity_y), 1 + 4 * parity_y

    end_x, end_y = lax.axis_size("gx") - 1, lax.axis_size("gy") - 1
    inner_x = jnp.where((gx == 0) | (gx == end_x), 0.0, 1.0)
    inner_y = jnp.where((gy == 0) | (gy == end_y), 0.0, 1.0)

    def put(x, y, block, factor=None):
        block = block.astype(F32)
        block = block if factor is None else block * factor
        window[x, y, 8:16, :] = block[0:8]
        window[x, y + 1, 8:16, :] = block[8:16]

    def put_one(x, y, block, factor=None):
        block = block.astype(F32)
        block = block if factor is None else block * factor
        for i in range(2):
            for j in range(2):
                first = (2 * i + j) * 4
                one_window[x + i, y + j, 8:12, :] = block[first:first + 4]

    for x in range(4):
        put(2 + x, 2, own_ref[x * 32:x * 32 + 16, :])
        put(2 + x, 4, own_ref[x * 32 + 16:x * 32 + 32, :])
    put_one(3, 3, own_ref[128:144, :])
    one = 1.0
    along_y = ((eveny_ref, even_y, one_even_y, one), (oddy_ref, odd_y, one_odd_y, inner_y))
    for got, y, one_y, factor in along_y:
        for x in range(4):
            put(2 + x, y, got[x * 16:x * 16 + 16, :], factor)
        put_one(3, one_y, got[64:80, :], factor)
    for got, place, one_x, factor_x in (
        (evenx_ref, even_x, one_even_x, one), (oddx_ref, odd_x, one_odd_x, inner_x)
    ):
        for x in range(2):
            put(place + x, 2, got[x * 32:x * 32 + 16, :], factor_x)
            put(place + x, 4, got[x * 32 + 16:x * 32 + 32, :], factor_x)
        put_one(one_x, 3, got[64:80, :], factor_x)
        for first, (_, y, one_y, factor_y) in zip((80, 128), along_y):
            for x in range(2):
                rows = slice(first + x * 16, first + x * 16 + 16)
                put(place + x, y, got[rows, :], factor_x * factor_y)
            put_one(one_x, one_y, got[first + 32:first + 48, :], factor_x * factor_y)


def translate_kernel(
    own_hbm, evenx_hbm, oddx_hbm, eveny_hbm, oddy_hbm,
    two_hbm, up_hbm, down_hbm, top_hbm, list_two_hbm, list_three_hbm, ops_hbm,
    out_ref, top_out,
    own_ref, evenx_ref, oddx_ref, eveny_ref, oddy_ref,
    two_ref, up_ref, down_ref, top_ref, list_two_ref, list_three_ref, fetch_sems,
    ops, window, one_window, chunks, one_chunks, high_chunks, two_rows, three_rows, acc,
    flags, one_local, sems,
):
    gx = lax.axis_index("gx")
    gy = lax.axis_index("gy")
    three_x, three_y = gx // 2, gy // 2
    copies = fetch(
        (own_hbm, evenx_hbm, oddx_hbm, eveny_hbm, oddy_hbm, two_hbm, up_hbm,
         list_two_hbm, list_three_hbm.at[three_x, three_y], down_hbm, top_hbm),
        (own_ref, evenx_ref, oddx_ref, eveny_ref, oddy_ref, two_ref, up_ref,
         list_two_ref, list_three_ref, down_ref, top_ref),
        fetch_sems,
    )
    def plane_copy(plane):
        span = pl.ds(PLANE_FIRST[plane], PLANE_COUNT[plane])
        return pltpu.make_async_copy(ops_hbm.at[span], ops.at[span], sems.at[plane])

    for plane in PLANE_ORDER[:2]:
        plane_copy(plane).start()

    window[:, :, 0:8, :] = jnp.zeros((8, 8, 8, PAIR), F32)
    window[:, :, 16:24, :] = jnp.zeros((8, 8, 8, PAIR), F32)
    one_window[...] = jnp.zeros_like(one_window)
    for copy in copies[:5]:
        copy.wait()
    window_of(window, one_window, own_ref, evenx_ref, oddx_ref, eveny_ref, oddy_ref)

    def fill(x, carry):
        for q in range(2):
            for d in range(3):
                for shift in range(3):
                    rows = pl.ds(7 + shift, 8)
                    both = [window[x, 2 * (y + d) + q, rows, :] for y in range(2)]
                    chunks[x, 3 * q + d, shift] = jnp.concatenate(both, axis=0).astype(BF16)
        return carry

    lax.fori_loop(0, 8, fill, 0)

    plane_copy(PLANE_ORDER[2]).start()
    for copy in copies[5:]:
        copy.wait()
    two_rows[...] = two_ref[...].astype(F32)
    cols = []
    for p in range(2):
        for q in range(2):
            for r in range(2):
                parts = []
                for x in range(4):
                    for z in range(2):
                        first = (2 * x + p) * 128 + q * 4 + 2 * z + r
                        parts.append(two_rows[pl.ds(first, 16, stride=8), :])
                cols.append(jnp.concatenate(parts, axis=0).astype(BF16))
    level_three = dot(jnp.concatenate(cols, axis=1), up_ref[...])
    three_rows[...] = level_three.astype(BF16).astype(F32)
    cols = []
    for p in range(2):
        for q in range(2):
            for r in range(2):
                parts = []
                for x in range(2):
                    first = ((2 * x + p) * 2 + r) * 16 + q
                    parts.append(three_rows[pl.ds(first, 8, stride=2), :])
                cols.append(jnp.concatenate(parts, axis=0).astype(BF16))
    top_out[...] = dot(jnp.concatenate(cols, axis=1), up_ref[...]).astype(BF16)

    flags[...] = jnp.zeros_like(flags)
    flags[0:4, :] = list_two_ref[...].astype(F32)
    flags[4:6, :] = list_three_ref[...].astype(F32)
    row = lax.broadcasted_iota(jnp.int32, (8, NOFF), 0)
    held = flags[...]
    moved = jnp.concatenate([jnp.zeros((8, 1), F32), held[:, :NOFF - 1]], axis=1)
    marked = jnp.where(row % 2 == 0, held, moved)
    row = lax.broadcasted_iota(jnp.int32, (8, COEF), 0)
    for plane in range(7):
        two_x = jnp.clip(gx + plane - 3, 0, 7)
        far_x = jnp.clip(three_x + plane - 3, 0, 3)
        for b in range(-3, 4):
            two_first = (two_x * 32 + jnp.clip(gy + b, 0, 31)) * 4
            far_first = far_x * 32 + jnp.clip(three_y + b, 0, 15)
            thin = plane in (2, 3, 4) and -1 <= b <= 1
            for r in range(2):
                low = two_rows[pl.ds(two_first + r, 1), :]
                high = two_rows[pl.ds(two_first + 2 + r, 1), :]
                far = three_rows[pl.ds(far_first + 16 * r, 1), :]
                low, high, far = (jnp.broadcast_to(v, (8, COEF)) for v in (low, high, far))
                near = jnp.where(row < 2, low, jnp.where(row < 4, high, far))
                for shift in range(3):
                    if thin and shift == 1:
                        continue
                    lane = lane_of(plane, b, 2 * (shift - 1) + r)
                    mark = jnp.broadcast_to(marked[:, lane:lane + 1], (8, COEF))
                    if shift == 0:
                        value = low
                    elif shift == 2:
                        value = high
                    else:
                        value = near
                    value = jnp.concatenate([value * mark, jnp.zeros((8, COEF), F32)], axis=0)
                    high_chunks[plane * 7 + b + 3, shift, :, r * COEF:r * COEF + COEF] = (
                        value.astype(BF16)
                    )

    acc[...] = jnp.zeros_like(acc)
    zero = jnp.zeros((COEF, COEF), BF16)

    def plane_step(plane, first, thin_plane, outer):
        a = plane - 3
        for b in range(-3, 4):
            for shift in range(3):
                for px in range(2):
                    for py in range(2):
                        rows = slice((2 * px + py) * 4, (2 * px + py) * 4 + 4)
                        one_chunks[b + 3, shift, rows, :] = one_window[
                            px + a + 3, py + b + 3, 7 + shift:11 + shift, :
                        ]
        parities = (jnp.where(a < 0, 1, 0),) if outer else (0, 1)
        places = [2 * x + px + a + 2 for px in parities for x in range(2)]
        size = 16 * len(places)
        totals = [None, None, None]
        for b in range(-3, 4):
            thin = thin_plane and -1 <= b <= 1
            start = first + (THIN_FIRST[b + 3] if thin_plane else 7 * (b + 3))
            sides = [py for py in range(2) if -2 <= b + py <= 3]
            left = []
            right = []
            for shift in (0, 2) if thin else (0, 1, 2):
                blocks = []
                for py in sides:
                    q, d = (py + b) % 2, (py + b) // 2 + 1
                    for place in places:
                        blocks.append(chunks[place, 3 * q + d, shift])
                blocks.append(one_chunks[b + 3, shift].astype(BF16))
                blocks.append(high_chunks[plane * 7 + b + 3, shift])
                left.append(jnp.concatenate(blocks, axis=0))
                if thin:
                    if shift == 0:
                        same, prev, after = ops[start + 1], ops[start], zero
                    else:
                        same, prev, after = ops[start + 2], zero, ops[start + 3]
                else:
                    c = 2 * (shift - 1) + 3
                    same, prev, after = ops[start + c], ops[start + c - 1], ops[start + c + 1]
                right.append(jnp.concatenate([same, prev], axis=1))
                right.append(jnp.concatenate([after, same], axis=1))
            product = dot(jnp.concatenate(left, axis=1), jnp.concatenate(right, axis=0))
            pieces = [product[i * size:(i + 1) * size] for i in range(len(sides))]
            pieces.append(product[len(sides) * size:])
            for side, piece in zip(sides + [2], pieces):
                totals[side] = piece if totals[side] is None else totals[side] + piece
        for side in range(2):
            if outer:
                rows = pl.ds(pl.multiple_of(side * 64 + parities[0] * 32, 32), 32)
            else:
                rows = slice(side * 64, side * 64 + 64)
            acc[rows, :] = acc[rows, :] + totals[side]
        acc[128:160, :] = acc[128:160, :] + totals[2]

    def thin_step(i, carry):
        first = 98 + 40 * i
        span = pl.ds(first, 40)
        pltpu.make_async_copy(ops_hbm.at[span], ops.at[span], sems.at[i + 2]).wait()
        ahead = pl.ds(jnp.where(i == 0, 49, jnp.where(i == 1, 218, 0)), 49)
        slot = jnp.where(i == 0, 1, jnp.where(i == 1, 5, 0))
        pltpu.make_async_copy(ops_hbm.at[ahead], ops.at[ahead], sems.at[slot]).start()
        plane_step(i + 2, first, True, False)
        return carry

    def wide_step(i, carry):
        plane = 1 + 4 * i
        first = 49 + 169 * i
        span = pl.ds(first, 49)
        pltpu.make_async_copy(ops_hbm.at[span], ops.at[span], sems.at[plane]).wait()
        plane_step(plane, first, False, False)
        return carry

    def outer_step(i, carry):
        plane = 6 * i
        first = 267 * i
        span = pl.ds(first, 49)
        pltpu.make_async_copy(ops_hbm.at[span], ops.at[span], sems.at[plane]).wait()
        plane_step(plane, first, False, True)
        return carry

    lax.fori_loop(0, 3, thin_step, 0)
    plane_copy(6).start()
    lax.fori_loop(0, 2, wide_step, 0)
    lax.fori_loop(0, 2, outer_step, 0)

    high = acc[144:152, :]
    top_x, top_y = three_x // 2, three_y // 2
    column = pl.multiple_of((three_x % 2 * 4 + three_y % 2 * 2) * COEF, PAIR)
    top_row = jnp.broadcast_to(top_ref[top_x, top_y], (8, COEF)).astype(BF16)
    three = dot(top_row, down_ref[:, pl.ds(column, PAIR)])
    row = lax.broadcasted_iota(jnp.int32, (8, COEF), 0)
    three_low = three[0:1, 0:COEF] + high[4:5, 0:COEF] * 0.125
    three_high = three[0:1, COEF:PAIR] + high[5:6, COEF:PAIR] * 0.125
    local_three = jnp.where(
        row == 0, jnp.broadcast_to(three_low, (8, COEF)), jnp.broadcast_to(three_high, (8, COEF))
    )
    column = pl.multiple_of((gx % 2 * 4 + gy % 2 * 2) * COEF, PAIR)
    two = dot(local_three.astype(BF16), down_ref[:, pl.ds(column, PAIR)])
    local_two = None
    for z in range(4):
        lanes = slice((z % 2) * COEF, (z % 2) * COEF + COEF)
        value = two[z // 2:z // 2 + 1, lanes] + high[z:z + 1, lanes] * 0.25
        value = jnp.broadcast_to(value, (8, COEF))
        local_two = value if local_two is None else jnp.where(row >= z, value, local_two)
    one = dot(local_two.astype(BF16), down_ref[...])
    one_mark = own_ref[272:288, :].astype(F32)
    for column in range(4):
        rows = slice(column * 4, column * 4 + 4)
        for r in range(2):
            lanes = slice(r * COEF, r * COEF + COEF)
            wide = slice((2 * column + r) * COEF, (2 * column + r) * COEF + COEF)
            far = acc[128 + column * 4:132 + column * 4, lanes] * one_mark[rows, lanes]
            one_local[pl.ds(column * 8 + r, 4, stride=2), :] = one[0:4, wide] + far * 0.5
    leaf = dot(one_local[...].astype(BF16), down_ref[...])
    leaf_mark = own_ref[144:272, :].astype(F32)
    for px in range(2):
        for py in range(2):
            for x in range(2):
                for y in range(2):
                    part = 8 * (2 * x + y)
                    held = ((2 * py + px) * 2 + x) * 16 + 8 * y
                    box_x, box_y = 2 * x + px, 2 * y + py
                    marked = box_x * 32 + box_y * 8
                    for r in range(2):
                        lanes = slice(r * COEF, r * COEF + COEF)
                        wide = slice((4 * px + 2 * py + r) * COEF, (4 * px + 2 * py + r + 1) * COEF)
                        mark = leaf_mark[marked:marked + 8, lanes]
                        out_ref[box_x, box_y, pl.ds(r, 8, stride=2), :] = (
                            leaf[part:part + 8, wide] + acc[held:held + 8, lanes] * mark
                        )


def translate(*operands):
    return pl.pallas_call(
        translate_kernel,
        out_shape=(
            jax.ShapeDtypeStruct((4, 4, 16, COEF), F32),
            jax.ShapeDtypeStruct((16, COEF), BF16),
        ),
        in_specs=[ANY_SPEC] * 12,
        out_specs=[VMEM_SPEC] * 2,
        scratch_shapes=[
            VM((288, PAIR), BF16),
            VM((176, PAIR), BF16),
            VM((176, PAIR), BF16),
            VM((80, PAIR), BF16),
            VM((80, PAIR), BF16),
            VM((1024, COEF), BF16),
            VM((1024, COEF), BF16),
            VM((COEF, 1024), BF16),
            VM((2, 8, 1, COEF), F32),
            VM((4, NOFF), jnp.int32),
            VM((2, NOFF), jnp.int32),
            pltpu.SemaphoreType.DMA((11,)),
            VM((NOFF, COEF, COEF), BF16),
            VM((8, 8, 24, PAIR), F32),
            VM((8, 8, 16, PAIR), F32),
            VM((8, 6, 3, 16, PAIR), BF16),
            VM((7, 3, 16, PAIR), F32),
            VM((49, 3, 16, PAIR), BF16),
            VM((1024, COEF), F32),
            VM((128, COEF), F32),
            VM((160, PAIR), F32),
            VM((8, NOFF), F32),
            VM((32, COEF), F32),
            pltpu.SemaphoreType.DMA((7,)),
        ],
        compiler_params=pltpu.CompilerParams(vmem_limit_bytes=int(LIM2 * 2**20)),
        name="translate",
    )(*operands)


def swaps(size_x, size_y):
    def odd(i):
        return ((i + 1) ^ 1) - 1

    every = [(x, y) for x in range(size_x) for y in range(size_y)]
    partners = (
        lambda x, y: (x ^ 1, y),
        lambda x, y: (odd(x) % size_x, y),
        lambda x, y: (x, y ^ 1),
        lambda x, y: (x, odd(y)) if 0 <= odd(y) < size_y else (x ^ 1, y),
    )
    place = lambda box: box[0] * size_y + box[1]
    return [[(place(box), place(partner(*box))) for box in every] for partner in partners]


def local(
    leaf_multipoles, top_local, upward_ops, downward_ops, translate_ops,
    interaction_leaf, interaction_one, interaction_two, interaction_three,
):
    count_x, count_y = lax.axis_size("gx"), lax.axis_size("gy")
    last = (1, 2, 3, 0)
    own, to_even, to_odd, two = prepare(
        count_x * count_y, leaf_multipoles, upward_ops, interaction_leaf.transpose(last), interaction_one.transpose(last)
    )
    axes = ("gx", "gy")
    pairs_even_x, pairs_odd_x, pairs_even_y, pairs_odd_y = swaps(count_x, count_y)
    even_y = lax.ppermute(to_even, axes, pairs_even_y)
    odd_y = lax.ppermute(to_odd, axes, pairs_odd_y)
    to_even, to_odd = forward(own, even_y, odd_y)
    even_x = lax.ppermute(to_even, axes, pairs_even_x)
    odd_x = lax.ppermute(to_odd, axes, pairs_odd_x)
    all_two = lax.all_to_all(two, axes, 0, 0, tiled=True).reshape(-1, COEF)
    leaf_local, top = translate(
        own, even_x, odd_x, even_y, odd_y,
        all_two, upward_ops, downward_ops, top_local,
        interaction_two.transpose(last).reshape(4, NOFF), interaction_three.transpose(last),
        translate_ops,
    )
    return leaf_local, top.reshape(2, 8, 1, COEF)


def solution(mesh):
    return jax.shard_map(
        local,
        mesh=mesh,
        in_specs=(
            P("gx", "gy", None, None),
            P(),
            P(),
            P(),
            P(),
            P(None, "gx", "gy", None),
            P(None, "gx", "gy", None),
            P(None, "gx", "gy", None),
            P(),
        ),
        out_specs=(P("gx", "gy", None, None), P()),
        check_vma=False,
    )
```

time: 53 us -> 44.5 us (0.84)
  local copies, waits for them, and re-layouts: 12.5 us -> 0.93 us
  Pallas kernels: 7.82 us -> 10.6 us
  waiting for transfers between devices: 10.8 us -> 11.5 us
    unnamed x20 -> x10, local copies, waits for them, and re-layouts: 11.7 us -> 0.93 us
    all_to_all x1, waiting for transfers between devices: 3.96 us -> 6.69 us  [local(): all_two = lax.all_to_all(two, axes, 0, 0, tiled=True).reshape(-1, COEF)]
    ppermute x4, waiting for transfers between devices: 6.88 us -> 4.77 us  [the longest x1 3.83 us: local(): odd_x = lax.ppermute(to_odd, axes, pairs_odd_x)]
    pallas_call x1, Pallas kernels: 0.33 us -> 2.27 us  [prepare(): pl.pallas_call(prepare_kernel, out_shape=(jax.ShapeDtypeStruct((288, PAIR...]
    ppermute x4, starting transfers between devices: 4.9 us -> 5.82 us  [the longest x1 2.55 us: local(): even_y = lax.ppermute(to_even, axes, pairs_even_y)]
    all_to_all x1, starting transfers between devices: 15.7 us -> 14.8 us  [local(): all_two = lax.all_to_all(two, axes, 0, 0, tiled=True).reshape(-1, COEF)]
    broadcast_in_dim x1 -> x0, local copies, waits for them, and re-layouts: 0.79 us -> none  [local(): copies = jnp.broadcast_to(two[None], (count_x * count_y, 4, COEF))]
    pallas_call x1, Pallas kernels: 7.48 us -> 8.27 us  [translate(): pl.pallas_call(translate_kernel, out_shape=(jax.ShapeDtypeStruct((4, 4, 1...]
where the time goes in v1:
time: 44.5 us; the launch traced here: 44.3 us
  starting transfers between devices  20.6 us (46%)
  waiting for transfers between devices  11.5 us (26%)
  Pallas kernels  10.6 us (24%)
  local copies, waits for them, and re-layouts  0.93 us (2%)
  between operations  0.71 us (2%)
    all_to_all x1, starting transfers between devices, local(): all_two = lax.all_to_all(two, axes, 0, 0, tiled=True).reshape(-1, COEF)  14.8 us
    pallas_call x1, Pallas kernels, translate(): pl.pallas_call(translate_kernel, out_shape=(jax.ShapeDtypeStruct((4, 4, 1...  8.27 us
    all_to_all x1, waiting for transfers between devices, local(): all_two = lax.all_to_all(two, axes, 0, 0, tiled=True).reshape(-1, COEF)  6.69 us
    ppermute x1, waiting for transfers between devices, local(): odd_x = lax.ppermute(to_odd, axes, pairs_odd_x)  3.83 us
    ppermute x1, starting transfers between devices, local(): even_y = lax.ppermute(to_even, axes, pairs_even_y)  2.55 us
    ppermute x1, starting transfers between devices, local(): even_x = lax.ppermute(to_even, axes, pairs_even_x)  2.31 us
    pallas_call x1, Pallas kernels, prepare(): pl.pallas_call(prepare_kernel, out_shape=(jax.ShapeDtypeStruct((288, PAIR...  2.27 us
    ppermute x1, starting transfers between devices, local(): odd_y = lax.ppermute(to_odd, axes, pairs_odd_y)  0.96 us
  transfers between devices with their start and end apart: 5, of which 3 were waited for; matrix products, arithmetic and copies ran while one was open for 0% of the time, Pallas kernels for 0%

profile of v1, /device:TPU:1, one launch (start us, length us, event | category | flops | bytes accessed | tf_op | source)
XLA Modules:
  0.0 44.3 jit_solution(6142191038730782389)
XLA Ops:
  0.6 2.3 %prepare.1 = (bf16[288,256]{1,0:T(8,128)(2,1)}, bf16[80,256]{1,0:T(8,128)(2,1)}, bf16[80,256]{1,0:T(8,128)(2,1)}, bf16[256,4,128]{2,1,0:T(4,128)(2,1)}) custom-call(bf16[4,4,16,128]{3,2,1,0:T(8,128)(2,1)} %leaf_hbm.1, bf16[1024,128]{1,0:T(8,128)(2,1)} %up_hbm.3, s32[4,4,16,316]{3,2,1,0:T(8,128)} %bitcast.10, s32[2,2,8,316]{3,2,1,0:T(8,128)} %bitcast.12), custom_call_target="tpu_custom_call" | custom-call | tf_op jit(solution)/shard_map/prepare/pallas_call | solution.py:125
  2.9 2.6 %collective-permute-start = (bf16[80,256]{1,0:T(8,128)(2,1)}, bf16[80,256]{1,0:T(8,128)(2,1)S(1)}, u32[]{:S(2)}, u32[]{:S(2)}) collective-permute-start(bf16[80,256]{1,0:T(8,128)(2,1)} %get-tuple-element.11), channel_id=1, source_target_pairs={{0,1},{1,0},{2,3},{3,2},{4,5},{5,4},{6,7},{7,6},{8,9},{9,8},{10,11... | collective-permute-start | bytes 122888 | tf_op jit(solution)/shard_map/ppermute | solution.py:543
  5.5 1.0 %collective-permute-start.1 = (bf16[80,256]{1,0:T(8,128)(2,1)}, bf16[80,256]{1,0:T(8,128)(2,1)S(1)}, u32[]{:S(2)}, u32[]{:S(2)}) collective-permute-start(bf16[80,256]{1,0:T(8,128)(2,1)} %get-tuple-element.12), channel_id=1, source_target_pairs={{0,32},{1,2},{2,1},{3,4},{4,3},{5,6},{6,5},{7,8},{8,7},{9,10},{10,... | collective-permute-start | bytes 122888 | tf_op jit(solution)/shard_map/ppermute | solution.py:544
  6.4 14.8 %all-to-all-start = ((bf16[256,4,128]{2,1,0:T(4,128)(2,1)}), bf16[256,4,128]{2,1,0:T(4,128)(2,1)}, u32[]{:S(2)}, u32[]{:S(2)}) async-start(bf16[256,4,128]{2,1,0:T(4,128)(2,1)} %get-tuple-element.15), calls=%async_computation | async-start | bytes 524288 | tf_op jit(solution)/shard_map/all_to_all | solution.py:548
  21.3 0.0 collective-permute-done.even_ref.eveny_hbm
  21.3 0.0 copy-start.1
  21.3 0.0 collective-permute-done.1.odd_ref.oddy_hbm
  21.3 0.0 copy-start.2
  21.3 0.0 copy-start
  21.3 0.9 %copy-done = bf16[288,256]{1,0:T(8,128)(2,1)S(1)} copy-done((bf16[288,256]{1,0:T(8,128)(2,1)S(1)}, bf16[288,256]{1,0:T(8,128)(2,1)}, u32[]{:S(2)}) %copy-start) | copy-done | bytes 147480
  22.2 0.0 copy-done.1
  22.2 0.0 copy-done.2
  22.3 2.3 %collective-permute-start.2 = (bf16[176,256]{1,0:T(8,128)(2,1)S(1)}, bf16[176,256]{1,0:T(8,128)(2,1)S(1)}, u32[]{:S(2)}, u32[]{:S(2)}) collective-permute-start(bf16[176,256]{1,0:T(8,128)(2,1)S(1)} %get-tuple-element.13), channel_id=1, source_target_pairs={{0,32},{1,33},{2,34},{3,35},{4,36},{5,37},{6,38},{7,39},{8,40},{9,... | collective-permute-start | bytes 270344 | tf_op jit(solution)/shard_map/ppermute | solution.py:546
  24.6 0.0 collective-permute-start.3
  24.6 0.9 %collective-permute-done.2.evenx_hbm = bf16[176,256]{1,0:T(8,128)(2,1)S(1)} collective-permute-done((bf16[176,256]{1,0:T(8,128)(2,1)S(1)}, bf16[176,256]{1,0:T(8,128)(2,1)S(1)}, u32[]{:S(2)}, u32[]{:S(2)}) %collective-permute-start.2) | collective-permute-done | bytes 90144 | tf_op jit(solution)/shard_map/ppermute | solution.py:546
  25.5 0.0 copy-start.3
  25.5 3.8 %collective-permute-done.3.oddx_hbm = bf16[176,256]{1,0:T(8,128)(2,1)S(1)} collective-permute-done((bf16[176,256]{1,0:T(8,128)(2,1)S(1)}, bf16[176,256]{1,0:T(8,128)(2,1)S(1)}, u32[]{:S(2)}, u32[]{:S(2)}) %collective-permute-start.3) | collective-permute-done | bytes 90144 | tf_op jit(solution)/shard_map/ppermute | solution.py:547
  29.3 0.0 copy-start.4
  29.3 6.7 %all-to-all-done = bf16[256,4,128]{2,1,0:T(4,128)(2,1)} async-done(((bf16[256,4,128]{2,1,0:T(4,128)(2,1)}), bf16[256,4,128]{2,1,0:T(4,128)(2,1)}, u32[]{:S(2)}, u32[]{:S(2)}) %all-to-all-start) | async-done | bytes 262176 | tf_op jit(solution)/shard_map/all_to_all | solution.py:548
  36.0 0.0 copy-done.3
  36.0 0.0 copy-done.4
  36.0 8.3 %translate.1 = (f32[4,4,16,128]{3,2,1,0:T(8,128)}, bf16[16,128]{1,0:T(8,128)(2,1)}) custom-call(bf16[288,256]{1,0:T(8,128)(2,1)} %get-tuple-element.10.own_ref.own_hbm, bf16[176,256]{1,0:T(8,128)(2,1)} %copy-done.3, bf16[176,256]{1,0:T(8,128)(2,1)} %copy-done.4, bf16[80,256]{1,0:T(8,128)(2,1)} %copy-done.1, bf16[80,256]{1,0:T(8,128)(2,1)} %copy-done.2, ...), custom_call_target="tpu_custom_call" | custom-call | tf_op jit(solution)/shard_map/translate/pallas_call | solution.py:478
  (1 shorter events, 0.0 us)
Async XLA Ops:
  2.9 18.3 %collective-permute-start = (bf16[80,256]{1,0:T(8,128)(2,1)}, bf16[80,256]{1,0:T(8,128)(2,1)S(1)}, u32[]{:S(2)}, u32[]{:S(2)}) collective-permute-start(bf16[80,256]{1,0:T(8,128)(2,1)} %get-tuple-element.11), channel_id=1, source_target_pairs={{0,1},{1,0},{2,3},{3,2},{4,5},{5,4},{6,7},{7,6},{8,9},{9,8},{10,11... | collective-permute-start | bytes 122888 | tf_op jit(solution)/shard_map/ppermute | solution.py:543
  5.5 15.8 %collective-permute-start.1 = (bf16[80,256]{1,0:T(8,128)(2,1)}, bf16[80,256]{1,0:T(8,128)(2,1)S(1)}, u32[]{:S(2)}, u32[]{:S(2)}) collective-permute-start(bf16[80,256]{1,0:T(8,128)(2,1)} %get-tuple-element.12), channel_id=1, source_target_pairs={{0,32},{1,2},{2,1},{3,4},{4,3},{5,6},{6,5},{7,8},{8,7},{9,10},{10,... | collective-permute-start | bytes 122888 | tf_op jit(solution)/shard_map/ppermute | solution.py:544
  6.4 29.6 %all-to-all-start = ((bf16[256,4,128]{2,1,0:T(4,128)(2,1)}), bf16[256,4,128]{2,1,0:T(4,128)(2,1)}, u32[]{:S(2)}, u32[]{:S(2)}) async-start(bf16[256,4,128]{2,1,0:T(4,128)(2,1)} %get-tuple-element.15), calls=%async_computation | async-start | bytes 524288 | tf_op jit(solution)/shard_map/all_to_all | solution.py:548
  21.3 1.0 %copy-start.1 = (bf16[80,256]{1,0:T(8,128)(2,1)}, bf16[80,256]{1,0:T(8,128)(2,1)S(1)}, u32[]{:S(2)}) copy-start(bf16[80,256]{1,0:T(8,128)(2,1)S(1)} %collective-permute-done.even_ref.eveny_hbm) | copy-start | bytes 122884
  21.3 1.0 %copy-start.2 = (bf16[80,256]{1,0:T(8,128)(2,1)}, bf16[80,256]{1,0:T(8,128)(2,1)S(1)}, u32[]{:S(2)}) copy-start(bf16[80,256]{1,0:T(8,128)(2,1)S(1)} %collective-permute-done.1.odd_ref.oddy_hbm) | copy-start | bytes 122884
  21.3 0.9 %copy-start = (bf16[288,256]{1,0:T(8,128)(2,1)S(1)}, bf16[288,256]{1,0:T(8,128)(2,1)}, u32[]{:S(2)}) copy-start(bf16[288,256]{1,0:T(8,128)(2,1)} %get-tuple-element.10.own_ref.own_hbm) | copy-start | bytes 442372
  22.3 3.2 %collective-permute-start.2 = (bf16[176,256]{1,0:T(8,128)(2,1)S(1)}, bf16[176,256]{1,0:T(8,128)(2,1)S(1)}, u32[]{:S(2)}, u32[]{:S(2)}) collective-permute-start(bf16[176,256]{1,0:T(8,128)(2,1)S(1)} %get-tuple-element.13), channel_id=1, source_target_pairs={{0,32},{1,33},{2,34},{3,35},{4,36},{5,37},{6,38},{7,39},{8,40},{9,... | collective-permute-start | bytes 270344 | tf_op jit(solution)/shard_map/ppermute | solution.py:546
  24.6 4.8 %collective-permute-start.3 = (bf16[176,256]{1,0:T(8,128)(2,1)S(1)}, bf16[176,256]{1,0:T(8,128)(2,1)S(1)}, u32[]{:S(2)}, u32[]{:S(2)}) collective-permute-start(bf16[176,256]{1,0:T(8,128)(2,1)S(1)} %get-tuple-element.14), channel_id=1, source_target_pairs={{0,224},{1,225},{2,226},{3,227},{4,228},{5,229},{6,230},{7,231},{8... | collective-permute-start | bytes 270344 | tf_op jit(solution)/shard_map/ppermute | solution.py:547
  25.5 10.5 %copy-start.3 = (bf16[176,256]{1,0:T(8,128)(2,1)}, bf16[176,256]{1,0:T(8,128)(2,1)S(1)}, u32[]{:S(2)}) copy-start(bf16[176,256]{1,0:T(8,128)(2,1)S(1)} %collective-permute-done.2.evenx_hbm) | copy-start | bytes 270340
  29.3 6.7 %copy-start.4 = (bf16[176,256]{1,0:T(8,128)(2,1)}, bf16[176,256]{1,0:T(8,128)(2,1)S(1)}, u32[]{:S(2)}) copy-start(bf16[176,256]{1,0:T(8,128)(2,1)S(1)} %collective-permute-done.3.oddx_hbm) | copy-start | bytes 270340

commit v2 on v1

--- a/solution.py
+++ b/solution.py
@@ -14,7 +14,7 @@
 NOFF = 316
 VM = pltpu.VMEM
 LIM1 = 60
-LIM2 = 60
+LIM2 = 46
 ANY_SPEC = pl.BlockSpec(memory_space=pl.ANY)
 VMEM_SPEC = pl.BlockSpec(memory_space=pltpu.VMEM)
 
@@ -170,7 +170,7 @@
         in_specs=[VMEM_SPEC] * 3,
         out_specs=[VMEM_SPEC] * 2,
         compiler_params=pltpu.CompilerParams(vmem_limit_bytes=4 * 2**20),
-        cost_estimate=pl.CostEstimate(flops=2 * 10**11, bytes_accessed=10**9, transcendentals=0),
+        cost_estimate=pl.CostEstimate(flops=10**11, bytes_accessed=0, transcendentals=0),
         name="forward",
     )(own, even, odd)
 
@@ -234,24 +234,15 @@
 
 
 def translate_kernel(
-    own_hbm, evenx_hbm, oddx_hbm, eveny_hbm, oddy_hbm,
-    two_hbm, up_hbm, down_hbm, top_hbm, list_two_hbm, list_three_hbm, ops_hbm,
+    own_ref, evenx_ref, oddx_ref, eveny_ref, oddy_ref,
+    two_ref, up_ref, down_ref, top_ref, list_two_ref, list_three_ref, ops_hbm,
     out_ref, top_out,
-    own_ref, evenx_ref, oddx_ref, eveny_ref, oddy_ref,
-    two_ref, up_ref, down_ref, top_ref, list_two_ref, list_three_ref, fetch_sems,
     ops, window, one_window, chunks, one_chunks, high_chunks, two_rows, three_rows, acc,
     flags, one_local, sems,
 ):
     gx = lax.axis_index("gx")
     gy = lax.axis_index("gy")
     three_x, three_y = gx // 2, gy // 2
-    copies = fetch(
-        (own_hbm, evenx_hbm, oddx_hbm, eveny_hbm, oddy_hbm, two_hbm, up_hbm,
-         list_two_hbm, list_three_hbm.at[three_x, three_y], down_hbm, top_hbm),
-        (own_ref, evenx_ref, oddx_ref, eveny_ref, oddy_ref, two_ref, up_ref,
-         list_two_ref, list_three_ref, down_ref, top_ref),
-        fetch_sems,
-    )
     def plane_copy(plane):
         span = pl.ds(PLANE_FIRST[plane], PLANE_COUNT[plane])
         return pltpu.make_async_copy(ops_hbm.at[span], ops.at[span], sems.at[plane])
@@ -262,8 +253,6 @@
     window[:, :, 0:8, :] = jnp.zeros((8, 8, 8, PAIR), F32)
     window[:, :, 16:24, :] = jnp.zeros((8, 8, 8, PAIR), F32)
     one_window[...] = jnp.zeros_like(one_window)
-    for copy in copies[:5]:
-        copy.wait()
     window_of(window, one_window, own_ref, evenx_ref, oddx_ref, eveny_ref, oddy_ref)
 
     def fill(x, carry):
@@ -278,8 +267,6 @@
     lax.fori_loop(0, 8, fill, 0)
 
     plane_copy(PLANE_ORDER[2]).start()
-    for copy in copies[5:]:
-        copy.wait()
     two_rows[...] = two_ref[...].astype(F32)
     cols = []
     for p in range(2):
@@ -306,7 +293,7 @@
 
     flags[...] = jnp.zeros_like(flags)
     flags[0:4, :] = list_two_ref[...].astype(F32)
-    flags[4:6, :] = list_three_ref[...].astype(F32)
+    flags[4:6, :] = list_three_ref[three_x, three_y].astype(F32)
     row = lax.broadcasted_iota(jnp.int32, (8, NOFF), 0)
     held = flags[...]
     moved = jnp.concatenate([jnp.zeros((8, 1), F32), held[:, :NOFF - 1]], axis=1)
@@ -481,21 +468,9 @@
             jax.ShapeDtypeStruct((4, 4, 16, COEF), F32),
             jax.ShapeDtypeStruct((16, COEF), BF16),
         ),
-        in_specs=[ANY_SPEC] * 12,
+        in_specs=[VMEM_SPEC] * 11 + [ANY_SPEC],
         out_specs=[VMEM_SPEC] * 2,
         scratch_shapes=[
-            VM((288, PAIR), BF16),
-            VM((176, PAIR), BF16),
-            VM((176, PAIR), BF16),
-            VM((80, PAIR), BF16),
-            VM((80, PAIR), BF16),
-            VM((1024, COEF), BF16),
-            VM((1024, COEF), BF16),
-            VM((COEF, 1024), BF16),
-            VM((2, 8, 1, COEF), F32),
-            VM((4, NOFF), jnp.int32),
-            VM((2, NOFF), jnp.int32),
-            pltpu.SemaphoreType.DMA((11,)),
             VM((NOFF, COEF, COEF), BF16),
             VM((8, 8, 24, PAIR), F32),
             VM((8, 8, 16, PAIR), F32),

time: 44.5 us -> 42.9 us (0.964)
  Pallas kernels: 10.6 us -> 8.98 us
  starting transfers between devices: 20.6 us -> 19.6 us
  waiting for transfers between devices: 11.5 us -> 12.5 us
    pallas_call x1, Pallas kernels: 8.27 us -> 6.68 us  [translate(): pl.pallas_call(translate_kernel, out_shape=(jax.ShapeDtypeStruct((4, 4, 1...]
    all_to_all x1, starting transfers between devices: 14.8 us -> 13.8 us  [local(): all_two = lax.all_to_all(two, axes, 0, 0, tiled=True).reshape(-1, COEF)]
    all_to_all x1, waiting for transfers between devices: 6.69 us -> 7.62 us  [local(): all_two = lax.all_to_all(two, axes, 0, 0, tiled=True).reshape(-1, COEF)]
    unnamed x10 -> x14, local copies, waits for them, and re-layouts: 0.93 us -> 0.93 us
where the time goes in v2:
time: 42.9 us; the launch traced here: 42.7 us
  starting transfers between devices  19.6 us (46%)
  waiting for transfers between devices  12.5 us (29%)
  Pallas kernels  8.98 us (21%)
  local copies, waits for them, and re-layouts  0.93 us (2%)
  between operations  0.73 us (2%)
    all_to_all x1, starting transfers between devices, local(): all_two = lax.all_to_all(two, axes, 0, 0, tiled=True).reshape(-1, COEF)  13.8 us
    all_to_all x1, waiting for transfers between devices, local(): all_two = lax.all_to_all(two, axes, 0, 0, tiled=True).reshape(-1, COEF)  7.62 us
    pallas_call x1, Pallas kernels, translate(): pl.pallas_call(translate_kernel, out_shape=(jax.ShapeDtypeStruct((4, 4, 1...  6.68 us
    ppermute x1, waiting for transfers between devices, local(): odd_x = lax.ppermute(to_odd, axes, pairs_odd_x)  3.96 us
    ppermute x1, starting transfers between devices, local(): even_y = lax.ppermute(to_even, axes, pairs_even_y)  2.55 us
    pallas_call x1, Pallas kernels, prepare(): pl.pallas_call(prepare_kernel, out_shape=(jax.ShapeDtypeStruct((288, PAIR...  2.27 us
    ppermute x1, starting transfers between devices, local(): even_x = lax.ppermute(to_even, axes, pairs_even_x)  2.23 us
    ppermute x1, starting transfers between devices, local(): odd_y = lax.ppermute(to_odd, axes, pairs_odd_y)  0.96 us
  transfers between devices with their start and end apart: 5, of which 3 were waited for; matrix products, arithmetic and copies ran while one was open for 0% of the time, Pallas kernels for 0%

profile of v2, /device:TPU:1, one launch (start us, length us, event | category | flops | bytes accessed | tf_op | source)
XLA Modules:
  0.0 42.7 jit_solution(8912783490868215355)
XLA Ops:
  0.6 2.3 %prepare.1 = (bf16[288,256]{1,0:T(8,128)(2,1)}, bf16[80,256]{1,0:T(8,128)(2,1)}, bf16[80,256]{1,0:T(8,128)(2,1)}, bf16[256,4,128]{2,1,0:T(4,128)(2,1)}) custom-call(bf16[4,4,16,128]{3,2,1,0:T(8,128)(2,1)} %leaf_hbm.1, bf16[1024,128]{1,0:T(8,128)(2,1)} %up_ref.1, s32[4,4,16,316]{3,2,1,0:T(8,128)} %bitcast.13, s32[2,2,8,316]{3,2,1,0:T(8,128)} %bitcast.14), custom_call_target="tpu_custom_call" | custom-call | tf_op jit(solution)/shard_map/prepare/pallas_call | solution.py:125
  2.9 2.6 %collective-permute-start = (bf16[80,256]{1,0:T(8,128)(2,1)}, bf16[80,256]{1,0:T(8,128)(2,1)S(1)}, u32[]{:S(2)}, u32[]{:S(2)}) collective-permute-start(bf16[80,256]{1,0:T(8,128)(2,1)} %get-tuple-element.11), channel_id=1, source_target_pairs={{0,1},{1,0},{2,3},{3,2},{4,5},{5,4},{6,7},{7,6},{8,9},{9,8},{10,11... | collective-permute-start | bytes 122888 | tf_op jit(solution)/shard_map/ppermute | solution.py:518
  5.5 1.0 %collective-permute-start.1 = (bf16[80,256]{1,0:T(8,128)(2,1)}, bf16[80,256]{1,0:T(8,128)(2,1)S(1)}, u32[]{:S(2)}, u32[]{:S(2)}) collective-permute-start(bf16[80,256]{1,0:T(8,128)(2,1)} %get-tuple-element.12), channel_id=1, source_target_pairs={{0,32},{1,2},{2,1},{3,4},{4,3},{5,6},{6,5},{7,8},{8,7},{9,10},{10,... | collective-permute-start | bytes 122888 | tf_op jit(solution)/shard_map/ppermute | solution.py:519
  6.4 13.8 %all-to-all-start = ((bf16[256,4,128]{2,1,0:T(4,128)(2,1)}), bf16[256,4,128]{2,1,0:T(4,128)(2,1)S(1)}, u32[]{:S(2)}, u32[]{:S(2)}) async-start(bf16[256,4,128]{2,1,0:T(4,128)(2,1)} %get-tuple-element.15), calls=%async_computation | async-start | bytes 524288 | tf_op jit(solution)/shard_map/all_to_all | solution.py:523
  20.3 0.0 collective-permute-done.even_ref.eveny_ref
  20.3 0.0 collective-permute-done.1.odd_ref.oddy_ref
  20.3 0.0 copy-start.3
  20.3 0.9 %copy-done.3 = bf16[288,256]{1,0:T(8,128)(2,1)S(1)} copy-done((bf16[288,256]{1,0:T(8,128)(2,1)S(1)}, bf16[288,256]{1,0:T(8,128)(2,1)}, u32[]{:S(2)}) %copy-start.3) | copy-done | bytes 147480
  21.2 0.0 copy-start
  21.2 0.0 copy-start.1
  21.2 0.0 copy-start.5
  21.2 0.0 copy-start.6
  21.3 2.2 %collective-permute-start.2 = (bf16[176,256]{1,0:T(8,128)(2,1)S(1)}, bf16[176,256]{1,0:T(8,128)(2,1)S(1)}, u32[]{:S(2)}, u32[]{:S(2)}) collective-permute-start(bf16[176,256]{1,0:T(8,128)(2,1)S(1)} %get-tuple-element.13), channel_id=1, source_target_pairs={{0,32},{1,33},{2,34},{3,35},{4,36},{5,37},{6,38},{7,39},{8,40},{9,... | collective-permute-start | bytes 270344 | tf_op jit(solution)/shard_map/ppermute | solution.py:521
  23.5 0.0 collective-permute-start.3
  23.5 0.9 %collective-permute-done.2.evenx_ref = bf16[176,256]{1,0:T(8,128)(2,1)S(1)} collective-permute-done((bf16[176,256]{1,0:T(8,128)(2,1)S(1)}, bf16[176,256]{1,0:T(8,128)(2,1)S(1)}, u32[]{:S(2)}, u32[]{:S(2)}) %collective-permute-start.2) | collective-permute-done | bytes 90144 | tf_op jit(solution)/shard_map/ppermute | solution.py:521
  24.4 4.0 %collective-permute-done.3.oddx_ref = bf16[176,256]{1,0:T(8,128)(2,1)S(1)} collective-permute-done((bf16[176,256]{1,0:T(8,128)(2,1)S(1)}, bf16[176,256]{1,0:T(8,128)(2,1)S(1)}, u32[]{:S(2)}, u32[]{:S(2)}) %collective-permute-start.3) | collective-permute-done | bytes 90144 | tf_op jit(solution)/shard_map/ppermute | solution.py:522
  28.4 7.6 %all-to-all-done = bf16[256,4,128]{2,1,0:T(4,128)(2,1)S(1)} async-done(((bf16[256,4,128]{2,1,0:T(4,128)(2,1)}), bf16[256,4,128]{2,1,0:T(4,128)(2,1)S(1)}, u32[]{:S(2)}, u32[]{:S(2)}) %all-to-all-start) | async-done | bytes 262176 | tf_op jit(solution)/shard_map/all_to_all | solution.py:523
  36.0 0.0 copy-done
  36.0 0.0 copy-done.1
  36.0 0.0 copy-done.2
  36.0 0.0 copy-done.4
  36.0 0.0 copy-done.5
  36.0 0.0 copy-done.6
  36.0 6.7 %translate.1 = (f32[4,4,16,128]{3,2,1,0:T(8,128)}, bf16[16,128]{1,0:T(8,128)(2,1)}) custom-call(bf16[288,256]{1,0:T(8,128)(2,1)S(1)} %copy-done.4, bf16[176,256]{1,0:T(8,128)(2,1)S(1)} %collective-permute-done.2.evenx_ref, bf16[176,256]{1,0:T(8,128)(2,1)S(1)} %collective-permute-done.3.oddx_ref, bf16[80,256]{1,0:T(8,128)(2,1)S(1)} %collective-permute-done.even_ref.eveny_ref, ...), custom_call_target="tpu_custom_call" | custom-call | tf_op jit(solution)/shard_map/translate/pallas_call | solution.py:465
  (3 shorter events, 0.0 us)
Async XLA Ops:
  2.9 17.3 %collective-permute-start = (bf16[80,256]{1,0:T(8,128)(2,1)}, bf16[80,256]{1,0:T(8,128)(2,1)S(1)}, u32[]{:S(2)}, u32[]{:S(2)}) collective-permute-start(bf16[80,256]{1,0:T(8,128)(2,1)} %get-tuple-element.11), channel_id=1, source_target_pairs={{0,1},{1,0},{2,3},{3,2},{4,5},{5,4},{6,7},{7,6},{8,9},{9,8},{10,11... | collective-permute-start | bytes 122888 | tf_op jit(solution)/shard_map/ppermute | solution.py:518
  5.5 14.8 %collective-permute-start.1 = (bf16[80,256]{1,0:T(8,128)(2,1)}, bf16[80,256]{1,0:T(8,128)(2,1)S(1)}, u32[]{:S(2)}, u32[]{:S(2)}) collective-permute-start(bf16[80,256]{1,0:T(8,128)(2,1)} %get-tuple-element.12), channel_id=1, source_target_pairs={{0,32},{1,2},{2,1},{3,4},{4,3},{5,6},{6,5},{7,8},{8,7},{9,10},{10,... | collective-permute-start | bytes 122888 | tf_op jit(solution)/shard_map/ppermute | solution.py:519
  6.4 29.6 %all-to-all-start = ((bf16[256,4,128]{2,1,0:T(4,128)(2,1)}), bf16[256,4,128]{2,1,0:T(4,128)(2,1)S(1)}, u32[]{:S(2)}, u32[]{:S(2)}) async-start(bf16[256,4,128]{2,1,0:T(4,128)(2,1)} %get-tuple-element.15), calls=%async_computation | async-start | bytes 524288 | tf_op jit(solution)/shard_map/all_to_all | solution.py:523
  20.3 0.9 %copy-start.3 = (bf16[288,256]{1,0:T(8,128)(2,1)S(1)}, bf16[288,256]{1,0:T(8,128)(2,1)}, u32[]{:S(2)}) copy-start(bf16[288,256]{1,0:T(8,128)(2,1)} %get-tuple-element.10.own_ref) | copy-start | bytes 442372
  21.2 14.8 %copy-start = (bf16[1024,128]{1,0:T(8,128)(2,1)S(1)}, bf16[1024,128]{1,0:T(8,128)(2,1)}, u32[]{:S(2)}) copy-start(bf16[1024,128]{1,0:T(8,128)(2,1)} %up_ref.1) | copy-start | bytes 786436
  21.2 14.8 %copy-start.1 = (bf16[128,1024]{1,0:T(8,128)(2,1)S(1)}, bf16[128,1024]{1,0:T(8,128)(2,1)}, u32[]{:S(2)}) copy-start(bf16[128,1024]{1,0:T(8,128)(2,1)} %down_ref.1) | copy-start | bytes 786436
  21.2 14.8 %copy-start.2 = (s32[316,4,16,2]{0,3,2,1:T(2,128)S(1)}, s32[316,4,16,2]{0,3,2,1:T(2,128)}, u32[]{:S(2)}) copy-start(s32[316,4,16,2]{0,3,2,1:T(2,128)} %param.17) | copy-start | bytes 485380
  21.2 14.8 %copy-start.4 = (bf16[288,256]{1,0:T(8,128)(2,1)S(1)}, bf16[288,256]{1,0:T(8,128)(2,1)}, u32[]{:S(2)}) copy-start(bf16[288,256]{1,0:T(8,128)(2,1)} %get-tuple-element.10.own_ref) | copy-start | bytes 442372
  21.2 14.8 %copy-start.5 = (f32[2,8,1,128]{3,2,1,0:T(1,128)S(1)}, f32[2,8,1,128]{3,2,1,0:T(1,128)}, u32[]{:S(2)}) copy-start(f32[2,8,1,128]{3,2,1,0:T(1,128)} %top_ref.1) | copy-start | bytes 24580
  21.2 14.8 %copy-start.6 = (s32[316,1,1,4]{0,3,2,1:T(4,128)S(1)}, s32[316,1,1,4]{0,3,2,1:T(4,128)}, u32[]{:S(2)}) copy-start(s32[316,1,1,4]{0,3,2,1:T(4,128)} %param.16) | copy-start | bytes 15172
  21.3 3.2 %collective-permute-start.2 = (bf16[176,256]{1,0:T(8,128)(2,1)S(1)}, bf16[176,256]{1,0:T(8,128)(2,1)S(1)}, u32[]{:S(2)}, u32[]{:S(2)}) collective-permute-start(bf16[176,256]{1,0:T(8,128)(2,1)S(1)} %get-tuple-element.13), channel_id=1, source_target_pairs={{0,32},{1,33},{2,34},{3,35},{4,36},{5,37},{6,38},{7,39},{8,40},{9,... | collective-permute-start | bytes 270344 | tf_op jit(solution)/shard_map/ppermute | solution.py:521
  23.5 4.9 %collective-permute-start.3 = (bf16[176,256]{1,0:T(8,128)(2,1)S(1)}, bf16[176,256]{1,0:T(8,128)(2,1)S(1)}, u32[]{:S(2)}, u32[]{:S(2)}) collective-permute-start(bf16[176,256]{1,0:T(8,128)(2,1)S(1)} %get-tuple-element.14), channel_id=1, source_target_pairs={{0,224},{1,225},{2,226},{3,227},{4,228},{5,229},{6,230},{7,231},{8... | collective-permute-start | bytes 270344 | tf_op jit(solution)/shard_map/ppermute | solution.py:522
